TPU v7x, 32 devices: a whole 2x2x4 slice. The times are simulated.
32 devices in a mesh: dp: 2 (over x), expert: 16 (over z, y, core).
Axes of the slice: x: 2, y: 2, z: 4, core: 2. Of those that a mesh axis runs over, the one named last changes fastest.
Arguments:
- tokens: bfloat16 [2048, 3584], P('expert'), may hold values from -6 to 6
- cotangent: bfloat16 [2048, 3584], P('expert'), may hold values from -0.59765625 to 0.59765625
- route_ids: int32 [2048, 8], P('expert'), may hold values from 0 to 15, all different within a row; in each aligned block of 128 rows (0 to 127, 128 to 255, ...) at most 80 rows name the same one
- route_gates: float32 [2048, 8], P('expert'), may hold values from 0.02 to 0.5
- w_gate: bfloat16 [16, 1792, 3584], P('expert', 'dp'), may hold values from -0.09375 to 0.09375
- w_up: bfloat16 [16, 1792, 3584], P('expert', 'dp'), may hold values from -0.09375 to 0.09375
- w_down: bfloat16 [16, 1792, 3584], P('expert', 'dp'), may hold values from -0.125 to 0.125
Outputs:
- layer_out: bfloat16 [2048, 3584], P(('expert', 'dp'))
- gate_grad: float32 [2048, 8], P(('expert', 'dp'))
- grad_w_gate: bfloat16 [16, 1792, 3584], P('expert', 'dp')
- grad_w_up: bfloat16 [16, 1792, 3584], P('expert', 'dp')
- grad_w_down: bfloat16 [16, 1792, 3584], P('expert', 'dp')
Inputs may be any that keep to these rules, and one draw needn't show every extreme that they name: `route_ids`: each row names 8 different experts. Within each aligned block of 128 rows (the tokens of one index of expert) no expert is named more than 80 times, a bound that some block reaches.
All inputs are finite; a program needn't handle non-finite values.
Results may differ from a plain program's by a relative error of at most 0.02.
Values may be sent and summed in bfloat16 or wider, within the bound.
A program may use at most 128 MiB of HBM per device.

v0:
```python
import jax
import jax.numpy as jnp
from jax import lax
from jax.sharding import PartitionSpec as P


def body(tokens, cotangent, route_ids, route_gates, w_gate, w_up, w_down):
    groups = lax.axis_size("expert")
    dp_count = lax.axis_size("dp")
    tok_rows, width = tokens.shape
    top_slots = route_ids.shape[1]
    cap_rows = min(tok_rows, dp_count * max(1, tok_rows * top_slots * 5 // (4 * groups * dp_count)))
    flat_ids = route_ids.reshape(-1)
    onehot = (flat_ids[:, None] == jnp.arange(groups, dtype=jnp.int32)[None, :]).astype(jnp.int32)
    slot_rank = jnp.sum(jnp.cumsum(onehot, axis=0) * onehot, axis=1) - 1
    rows_x = jnp.repeat(tokens, top_slots, axis=0)
    scaled = (route_gates[:, :, None] * cotangent[:, None, :].astype(jnp.float32)).astype(
        jnp.bfloat16
    )
    scaled = scaled.reshape(tok_rows * top_slots, width)
    send_x = jnp.zeros((groups, cap_rows, width), jnp.bfloat16).at[flat_ids, slot_rank].set(rows_x)
    send_dy = jnp.zeros((groups, cap_rows, width), jnp.bfloat16).at[flat_ids, slot_rank].set(scaled)
    recv_x, recv_dy = (
        lax.all_to_all(send_x, "expert", split_axis=0, concat_axis=0, tiled=True),
        lax.all_to_all(send_dy, "expert", split_axis=0, concat_axis=0, tiled=True),
    )
    rows_all = groups * cap_rows
    flat_x = recv_x.reshape(rows_all, width)
    flat_dy = recv_dy.reshape(rows_all, width)
    gate_local = w_gate[0]
    up_local = w_up[0]
    down_local = w_down[0]
    by_feature = (((1,), (1,)), ((), ()))
    by_row = (((0,), (0,)), ((), ()))
    gate_pre = lax.dot_general(flat_x, gate_local, by_feature, preferred_element_type=jnp.float32)
    up_pre = lax.dot_general(flat_x, up_local, by_feature, preferred_element_type=jnp.float32)
    sigma_gate = jax.nn.sigmoid(gate_pre)
    hidden = (gate_pre * sigma_gate * up_pre).astype(jnp.bfloat16)
    y_part = jnp.dot(hidden, down_local, preferred_element_type=jnp.float32).astype(jnp.bfloat16)
    hidden_grad = lax.dot_general(
        flat_dy, down_local, by_feature, preferred_element_type=jnp.float32
    )
    grad_gate_pre = (
        hidden_grad * up_pre * sigma_gate * (1.0 + gate_pre * (1.0 - sigma_gate))
    ).astype(jnp.bfloat16)
    grad_up_pre = (hidden_grad * gate_pre * sigma_gate).astype(jnp.bfloat16)
    grad_down = lax.dot_general(hidden, flat_dy, by_row, preferred_element_type=jnp.float32)
    grad_gate = lax.dot_general(grad_gate_pre, flat_x, by_row, preferred_element_type=jnp.float32)
    grad_up = lax.dot_general(grad_up_pre, flat_x, by_row, preferred_element_type=jnp.float32)
    y_flat, grad_gate, grad_up, grad_down = (y_part, grad_gate, grad_up, grad_down)
    y_home = lax.all_to_all(
        y_flat.reshape(groups, cap_rows, width), "expert", split_axis=0, concat_axis=0, tiled=True
    )
    y_slots = y_home[flat_ids, slot_rank].reshape(tok_rows, top_slots, width)
    out_part = jnp.einsum("tk,tkd->td", route_gates, y_slots, preferred_element_type=jnp.float32)
    grad_part = jnp.einsum("td,tkd->tk", cotangent, y_slots, preferred_element_type=jnp.float32)
    layer_sum, gate_sum = (
        lax.psum_scatter(
            out_part.astype(jnp.bfloat16), "dp", scatter_dimension=0, tiled=True
        ).astype(jnp.float32),
        lax.psum_scatter(
            grad_part.astype(jnp.bfloat16), "dp", scatter_dimension=0, tiled=True
        ).astype(jnp.float32),
    )
    return (
        layer_sum.astype(jnp.bfloat16),
        gate_sum,
        grad_gate.astype(jnp.bfloat16)[None],
        grad_up.astype(jnp.bfloat16)[None],
        grad_down.astype(jnp.bfloat16)[None],
    )


def solution(mesh):
    return jax.shard_map(
        body,
        mesh=mesh,
        in_specs=(
            P("expert", None),
            P("expert", None),
            P("expert", None),
            P("expert", None),
            P("expert", "dp", None),
            P("expert", "dp", None),
            P("expert", "dp", None),
        ),
        out_specs=(
            P(("expert", "dp"), None),
            P(("expert", "dp"), None),
            P("expert", "dp", None),
            P("expert", "dp", None),
            P("expert", "dp", None),
        ),
        check_vma=False,
    )
```

profile of v0, /device:TPU:0, one launch (start us, length us, event | category | flops | bytes accessed | tf_op | source)
XLA Modules:
  0.0 724.6 jit_solution(9439360295542455663)
XLA Ops:
  7.2 0.0 copy-start
  7.2 0.9 copy.20
  8.0 0.1 eq.29
  8.1 0.1 eq.25
  8.2 0.1 reshape.100
  8.3 4.5 reduce-window.6
  12.9 0.1 slice.10
  12.9 0.1 copy.23
  13.1 0.1 copy.24
  13.2 0.1 broadcast_add_fusion
  13.4 0.7 multiply_reduce_fusion
  14.1 0.8 and_reduce_fusion
  14.9 0.0 copy-done
  14.9 15.2 %scatter_custom_fusion = bf16[1280,3584]{1,0:T(8,128)(2,1)} fusion(s32[1024]{0:T(1024)S(1)} %broadcast_select_fusion, bf16[]{:T(256)} %constant.6.clone.1, bf16[128,3584]{1,0:T(8,128)(2,1)S(1)} %copy-done), kind=kCustom, calls=%fused_computation.11 | custom fusion | bytes 10092546
  30.1 0.0 copy-start.2
  30.1 0.0 copy-start.3
  30.1 7.7 %all-to-all-start = ((bf16[16,80,3584]{2,1,0:T(8,128)(2,1)}), bf16[16,80,3584]{2,1,0:T(8,128)(2,1)}, u32[]{:S(2)}, u32[]{:S(2)}) async-start(bf16[16,80,3584]{2,1,0:T(8,128)(2,1)} %bitcast.74), calls=%async_computation | async-start | bytes 18350080 | tf_op jit(solution)/shard_map/all_to_all | solution.py:24
  37.9 0.0 copy-done.2
  37.9 0.2 convert_element_type.51
  38.0 0.0 copy-done.3
  38.1 0.1 copy.25
  38.2 0.1 mul.48
  38.3 15.7 %scatter_custom_fusion.1 = bf16[1280,3584]{1,0:T(8,128)(2,1)} fusion(s32[1024]{0:T(1024)S(1)} %broadcast_select_fusion, f32[128,3584]{1,0:T(8,128)S(1)} %convert_element_type.51, f32[1024]{0:T(1024)S(1)} %mul.48, bf16[]{:T(256)} %constant.6.clone.1), kind=kCustom, calls=%fused_computation.6 | custom fusion | flops 7340032 | bytes 11014146
  53.9 148.3 %all-to-all-done = bf16[16,80,3584]{2,1,0:T(8,128)(2,1)} async-done(((bf16[16,80,3584]{2,1,0:T(8,128)(2,1)}), bf16[16,80,3584]{2,1,0:T(8,128)(2,1)}, u32[]{:S(2)}, u32[]{:S(2)}) %all-to-all-start) | async-done | bytes 9175072 | tf_op jit(solution)/shard_map/all_to_all | solution.py:24
  202.2 39.9 %all-to-all-start.2 = ((bf16[16,80,3584]{2,1,0:T(8,128)(2,1)}), bf16[16,80,3584]{2,1,0:T(8,128)(2,1)}, u32[]{:S(2)}, u32[]{:S(2)}) async-start(bf16[16,80,3584]{2,1,0:T(8,128)(2,1)} %bitcast.73), calls=%async_computation.3 | async-start | bytes 18350080 | tf_op jit(solution)/shard_map/all_to_all | solution.py:25
  242.2 0.0 slice-start
  242.2 13.6 %fusion.16 = f32[1280,896]{1,0:T(8,128)S(1)} fusion(bf16[1280,3584]{1,0:T(8,128)(2,1)} %bitcast.6, bf16[1,896,3584]{2,1,0:T(8,128)(2,1)} %param.11), kind=kOutput, calls=%fused_computation.23 | convolution fusion | flops 8220835840 | bytes 20185088 | tf_op jit(solution)/shard_map/dot_general | solution.py:35
  255.7 0.0 copy-start.4
  255.8 0.0 slice-start.1
  255.8 17.7 %multiply_convert_fusion.2 = (bf16[1280,896]{1,0:T(8,128)(2,1)}, f32[1280,896]{1,0:T(8,128)}) fusion(f32[1280,896]{1,0:T(8,128)S(1)} %fusion.16, bf16[1280,3584]{1,0:T(8,128)(2,1)} %bitcast.6, bf16[1,896,3584]{2,1,0:T(8,128)(2,1)} %param.12), kind=kOutput, calls=%fused_computation.32 | convolution fusion | flops 8227717120 | bytes 27066368 | tf_op jit(solution)/shard_map/dot_general | solution.py:36
  273.5 0.0 copy-done.4
  273.5 0.0 slice-done
  273.5 0.0 slice-done.1
  273.5 13.8 %convolution_convert_fusion = bf16[1280,3584]{1,0:T(8,128)(2,1)} fusion(bf16[1280,896]{1,0:T(8,128)(2,1)} %get-tuple-element.10, bf16[1,896,3584]{2,1,0:T(8,128)(2,1)S(1)} %bitcast.85), kind=kOutput, calls=%fused_computation.3 | convolution fusion | flops 8225423360 | bytes 17891328 | tf_op jit(solution)/shard_map/dot_general | solution.py:39
  287.3 119.3 %all-to-all-done.2 = bf16[16,80,3584]{2,1,0:T(8,128)(2,1)} async-done(((bf16[16,80,3584]{2,1,0:T(8,128)(2,1)}), bf16[16,80,3584]{2,1,0:T(8,128)(2,1)}, u32[]{:S(2)}, u32[]{:S(2)}) %all-to-all-start.2) | async-done | bytes 9175072 | tf_op jit(solution)/shard_map/all_to_all | solution.py:25
  406.6 39.7 %all-to-all-start.1 = ((bf16[16,80,3584]{2,1,0:T(8,128)(2,1)}), bf16[16,80,3584]{2,1,0:T(8,128)(2,1)}, u32[]{:S(2)}, u32[]{:S(2)}) async-start(bf16[16,80,3584]{2,1,0:T(8,128)(2,1)} %bitcast.75), calls=%async_computation.1 | async-start | bytes 18350080 | tf_op jit(solution)/shard_map/all_to_all | solution.py:51
  446.2 0.4 reduce-scatter.7.cloned.1.call-start
  446.7 0.1 copy.26
  446.9 13.4 %fusion.11 = f32[1280,896]{1,0:T(8,128)S(1)} fusion(bf16[1280,3584]{1,0:T(8,128)(2,1)} %bitcast.19, bf16[1,896,3584]{2,1,0:T(8,128)(2,1)} %param.13), kind=kOutput, calls=%fused_computation.18 | convolution fusion | flops 8220835840 | bytes 20185088 | tf_op jit(solution)/shard_map/dot_general | solution.py:40
  460.3 14.7 %fusion.19 = bf16[1,896,3584]{2,1,0:T(8,128)(2,1)} fusion(bf16[1280,3584]{1,0:T(8,128)(2,1)} %bitcast.6, f32[1280,896]{1,0:T(8,128)S(1)} %fusion.11, f32[1280,896]{1,0:T(8,128)} %copy-done.4), kind=kOutput, calls=%fused_computation.26 | convolution fusion | flops 8230928384 | bytes 24772608 | tf_op jit(solution)/shard_map/dot_general | solution.py:49
  474.9 17.8 %fusion.18 = bf16[1,896,3584]{2,1,0:T(8,128)(2,1)} fusion(bf16[1280,3584]{1,0:T(8,128)(2,1)} %bitcast.6, f32[1280,896]{1,0:T(8,128)} %copy-done.4, f32[1280,896]{1,0:T(8,128)S(1)} %fusion.11, f32[1280,896]{1,0:T(8,128)} %get-tuple-element.11), kind=kOutput, calls=%fused_computation.25 | convolution fusion | flops 8235515904 | bytes 29360128 | tf_op jit(solution)/shard_map/dot_general | solution.py:48
  492.8 117.9 %all-to-all-done.1 = bf16[16,80,3584]{2,1,0:T(8,128)(2,1)} async-done(((bf16[16,80,3584]{2,1,0:T(8,128)(2,1)}), bf16[16,80,3584]{2,1,0:T(8,128)(2,1)}, u32[]{:S(2)}, u32[]{:S(2)}) %all-to-all-start.1) | async-done | bytes 9175072 | tf_op jit(solution)/shard_map/all_to_all | solution.py:51
  610.7 32.5 %gather_fusion = bf16[1024,3584]{1,0:T(8,128)(2,1)} fusion(bf16[16,80,3584]{2,1,0:T(8,128)(2,1)} %all-to-all-done.1, s32[1024]{0:T(1024)S(1)} %bitcast.72), kind=kCustom, calls=%fused_computation | custom fusion | bytes 14688256 | tf_op jit(solution)/shard_map/gather | solution.py:54
  643.1 7.2 fusion.3
  650.4 0.1 copy.29
  650.4 0.7 copy.30
  651.2 0.0 reduce-scatter.7.cloned.1.call-update
  651.2 0.0 copy-start.5
  651.2 0.3 reduce-scatter.5.cloned.1.call-start
  651.5 5.3 fusion.5
  656.7 1.0 copy.37
  657.8 0.0 reduce-scatter.5.cloned.1.call-update
  657.8 0.0 copy-done.5
  657.8 0.0 copy-start.1
  657.8 12.9 %fusion.20 = bf16[1,896,3584]{2,1,0:T(8,128)(2,1)} fusion(bf16[1280,896]{1,0:T(8,128)(2,1)S(1)} %copy-done.5, bf16[1280,3584]{1,0:T(8,128)(2,1)} %bitcast.19), kind=kOutput, calls=%fused_computation.27 | convolution fusion | flops 8224047104 | bytes 17891328 | tf_op jit(solution)/shard_map/dot_general | solution.py:47
  670.8 25.0 %reduce-scatter.7.cloned.1.call-done = bf16[64,8]{1,0:T(8,128)(2,1)} async-done(((bf16[128,8]{1,0:T(8,128)(2,1)}), bf16[64,8]{1,0:T(8,128)(2,1)}) %reduce-scatter.7.cloned.1.call-update) | async-done | bytes 1040
  695.8 0.8 copy.31
  696.6 0.6 convert_element_type.50
  697.2 20.3 %reduce-scatter.5.cloned.1.call-done = bf16[64,3584]{1,0:T(8,128)(2,1)} async-done(((bf16[128,3584]{1,0:T(8,128)(2,1)}), bf16[64,3584]{1,0:T(8,128)(2,1)}) %reduce-scatter.5.cloned.1.call-update) | async-done | bytes 458768 | tf_op jit(solution)/shard_map/reduce_scatter | solution.py:58
  717.5 0.0 copy-done.1
  (8 shorter events, 0.1 us)
Async XLA Ops:
  7.2 7.7 %copy-start = (bf16[128,3584]{1,0:T(8,128)(2,1)S(1)}, bf16[128,3584]{1,0:T(8,128)(2,1)}, u32[]{:S(2)}) copy-start(bf16[128,3584]{1,0:T(8,128)(2,1)} %param.7) | copy-start | bytes 2752516
  30.1 7.8 %copy-start.2 = (bf16[128,3584]{1,0:T(8,128)(2,1)S(1)}, bf16[128,3584]{1,0:T(8,128)(2,1)}, u32[]{:S(2)}) copy-start(bf16[128,3584]{1,0:T(8,128)(2,1)} %param.8) | copy-start | bytes 2752516
  30.1 8.0 %copy-start.3 = (f32[128,8]{0,1:T(8,128)S(1)}, f32[128,8]{0,1:T(8,128)}, u32[]{:S(2)}) copy-start(f32[128,8]{0,1:T(8,128)} %param.10) | copy-start | bytes 12292
  30.1 172.1 %all-to-all-start = ((bf16[16,80,3584]{2,1,0:T(8,128)(2,1)}), bf16[16,80,3584]{2,1,0:T(8,128)(2,1)}, u32[]{:S(2)}, u32[]{:S(2)}) async-start(bf16[16,80,3584]{2,1,0:T(8,128)(2,1)} %bitcast.74), calls=%async_computation | async-start | bytes 18350080 | tf_op jit(solution)/shard_map/all_to_all | solution.py:24
  202.2 204.3 %all-to-all-start.2 = ((bf16[16,80,3584]{2,1,0:T(8,128)(2,1)}), bf16[16,80,3584]{2,1,0:T(8,128)(2,1)}, u32[]{:S(2)}, u32[]{:S(2)}) async-start(bf16[16,80,3584]{2,1,0:T(8,128)(2,1)} %bitcast.73), calls=%async_computation.3 | async-start | bytes 18350080 | tf_op jit(solution)/shard_map/all_to_all | solution.py:25
  242.2 31.3 %slice-start = ((s8[6422528]{0:T(1024)(128)(4,1)}), s8[4194304]{0:T(1024)(128)(4,1)S(1)}, s32[]{:S(2)}) async-start(s8[6422528]{0:T(1024)(128)(4,1)} %bitcast.84), calls=%async_computation.7 | async-start | bytes 8388608
  255.7 17.7 %copy-start.4 = (f32[1280,896]{1,0:T(8,128)}, f32[1280,896]{1,0:T(8,128)S(1)}, u32[]{:S(2)}) copy-start(f32[1280,896]{1,0:T(8,128)S(1)} %fusion.16) | copy-start | bytes 13762564
  255.8 17.7 %slice-start.1 = ((s8[6422528]{0:T(1024)(128)(4,1)}), s8[2228224]{0:T(1024)(128)(4,1)S(1)}, s32[]{:S(2)}) async-start(s8[6422528]{0:T(1024)(128)(4,1)} %bitcast.84), calls=%async_computation.8 | async-start | bytes 4456448
  406.6 204.1 %all-to-all-start.1 = ((bf16[16,80,3584]{2,1,0:T(8,128)(2,1)}), bf16[16,80,3584]{2,1,0:T(8,128)(2,1)}, u32[]{:S(2)}, u32[]{:S(2)}) async-start(bf16[16,80,3584]{2,1,0:T(8,128)(2,1)} %bitcast.75), calls=%async_computation.1 | async-start | bytes 18350080 | tf_op jit(solution)/shard_map/all_to_all | solution.py:51
  446.2 249.5 %reduce-scatter.7.cloned.1.call-start = ((), (), s32[]{:S(2)}) async-start(), calls=%async_computation.6 | async-start | bytes 49152
  651.2 6.6 copy-start.5
  651.2 66.3 %reduce-scatter.5.cloned.1.call-start = ((), (), s32[]{:S(2)}) async-start(), calls=%async_computation.5 | async-start | bytes 1376256 | tf_op jit(solution)/shard_map/reduce_scatter | solution.py:58
  657.8 59.7 %copy-start.1 = (bf16[128,3584]{1,0:T(8,128)(2,1)S(1)}, bf16[128,3584]{1,0:T(8,128)(2,1)}, u32[]{:S(2)}) copy-start(bf16[128,3584]{1,0:T(8,128)(2,1)} %param.7) | copy-start | bytes 2752516
Sparse Core Ops, SparseCore 0:
  651.3 44.4 reduce-scatter.6
  698.6 18.8 reduce-scatter.4
where the time goes:
time: 733 us; the launch traced here: 725 us
  waiting for transfers between devices  431 us (59%)
  matrix products  116 us (16%)
  starting transfers between devices  88 us (12%)
  local copies, waits for them, and re-layouts  52.2 us (7%)
  other arithmetic  22.7 us (3%)
  between operations  14.5 us (2%)
    all_to_all x1, waiting for transfers between devices, body(): lax.all_to_all(send_x, 'expert', split_axis=0, concat_axis=0, tiled=True)  148 us
    all_to_all x1, waiting for transfers between devices, body(): lax.all_to_all(send_dy, 'expert', split_axis=0, concat_axis=0, tiled=True)  119 us
    all_to_all x1, waiting for transfers between devices, body(): lax.all_to_all(y_flat.reshape(groups, cap_rows, width), 'expert', split_a...  118 us
    all_to_all x1, starting transfers between devices, body(): lax.all_to_all(send_dy, 'expert', split_axis=0, concat_axis=0, tiled=True)  39.9 us
    all_to_all x1, starting transfers between devices, body(): lax.all_to_all(y_flat.reshape(groups, cap_rows, width), 'expert', split_a...  39.7 us
    gather x1, local copies, waits for them, and re-layouts, body(): y_slots = y_home[flat_ids, slot_rank].reshape(tok_rows, top_slots, width)  32.5 us
    unnamed x3, waiting for transfers between devices  25 us
    reduce_scatter x1, waiting for transfers between devices, body(): lax.psum_scatter(out_part.astype(jnp.bfloat16), 'dp', scatter_dimension=0...  20.3 us
  transfers between devices with their start and end apart: 5, of which 5 were waited for; matrix products, arithmetic and copies ran while one was open for 18% of the time, Pallas kernels for 0%

commit v1 on v0

v1 whole, which is shorter than its diff:
```python
import jax
import jax.numpy as jnp
from jax import lax
from jax.sharding import PartitionSpec as P

BY_FEATURE = (((1,), (1,)), ((), ()))
BY_ROW = (((0,), (0,)), ((), ()))


def swap(a, axis, bits):
    size = lax.axis_size(axis)
    return lax.ppermute(a, axis, [(i, i ^ bits) for i in range(size)])


def collect(a):
    dp_count = lax.axis_size("dp")
    z_count = lax.axis_size("expert") // 4
    rows, width = a.shape
    a = jnp.stack([a] + [swap(a, "expert", 4 * z) for z in range(1, z_count)])
    first = a[:, None, None, None, : rows // 2]
    second = a[:, None, None, None, rows // 2 :]

    def along_y(b):
        return jnp.concatenate([b, swap(b, "expert", 2)], axis=1)

    def along_dp(b):
        return jnp.concatenate([b] + [swap(b, "dp", d) for d in range(1, dp_count)], axis=3)

    both = jnp.concatenate([along_y(along_dp(first)), along_dp(along_y(second))], axis=2)
    return both.reshape(2 * z_count, dp_count * rows, width)


def hand_back(a, rows):
    dp_count = lax.axis_size("dp")
    z_count = lax.axis_size("expert") // 4
    width = a.shape[-1]
    a = a.reshape(z_count, 2, 2, dp_count, rows // 2, width)

    def total(parts):
        return sum(p.astype(jnp.float32) for p in parts).astype(jnp.bfloat16)

    def along_y(b):
        return total([b[:, :1], swap(b[:, 1:], "expert", 2)])

    def along_dp(b):
        return total([b[:, :, :1]] + [swap(b[:, :, d : d + 1], "dp", d) for d in range(1, dp_count)])

    first = along_dp(along_y(a[:, :, 0]))
    second = along_y(along_dp(a[:, :, 1]))
    both = jnp.concatenate([first, second], axis=3).reshape(z_count, rows, width)
    return total([both[0]] + [swap(both[z], "expert", 4 * z) for z in range(1, z_count)])


def body(tokens, cotangent, route_ids, route_gates, w_gate, w_up, w_down):
    groups = lax.axis_size("expert")
    dp_count = lax.axis_size("dp")
    me = lax.axis_index("expert")
    part = lax.axis_index("dp")
    tok_rows, width = tokens.shape
    top_slots = route_ids.shape[1]
    cap_rows = min(tok_rows, dp_count * max(1, tok_rows * top_slots * 5 // (4 * groups * dp_count)))
    own_rows = tok_rows // dp_count
    near = groups // 2

    def share(a):
        return lax.dynamic_slice_in_dim(a, part * own_rows, own_rows, 0)

    experts = jnp.arange(groups, dtype=jnp.int32)
    named = route_ids[:, :, None] == experts[None, None, :]
    gates = jnp.sum(jnp.where(named, route_gates[:, :, None], 0.0), axis=1)
    gates = lax.all_gather(gates, "expert", tiled=True)

    block = jnp.arange(groups * dp_count, dtype=jnp.int32)
    partner = (block // dp_count ^ me) * dp_count + (block % dp_count ^ part)
    partner = (partner[:, None] == block[None, :])[:, :, None]

    def reorder(a):
        return jnp.sum(jnp.where(partner, a.reshape(1, -1, own_rows), 0.0), axis=1)

    def near_far(expert):
        a = jnp.sum(jnp.where(experts == expert, gates, 0.0), axis=1)
        a = reorder(a).reshape(near, 2, dp_count, 2, own_rows // 2)
        return a.transpose(1, 0, 3, 2, 4).reshape(2, near, tok_rows)

    upto = jnp.triu(jnp.ones((tok_rows, tok_rows), jnp.bfloat16))
    places = jnp.arange(cap_rows, dtype=jnp.float32)

    def slots(a):
        chosen = a > 0
        count = jnp.dot(chosen.astype(jnp.bfloat16), upto, preferred_element_type=jnp.float32)
        rank = jnp.where(chosen, count - 1.0, -1.0)
        return rank[..., None, :] == places[:, None]

    own_gates = near_far(me)
    own_pick = slots(own_gates)
    gate_slot = jnp.sum(jnp.where(own_pick, own_gates[:, :, None, :], 0.0), axis=3).reshape(-1, 1)
    pair_pick = slots(near_far(me ^ 1)[0])
    pick = jnp.concatenate([own_pick[0], pair_pick], axis=1).astype(jnp.bfloat16)

    def to_slots(a):
        a = collect(share(a))
        rows = jnp.einsum("gct,gtd->gcd", pick[:, cap_rows:], a, preferred_element_type=jnp.float32)
        sent = swap(rows.astype(jnp.bfloat16), "expert", 1)
        rows = jnp.einsum("gct,gtd->gcd", pick[:, :cap_rows], a, preferred_element_type=jnp.float32)
        return jnp.concatenate([rows.astype(jnp.bfloat16), sent]).reshape(-1, width)

    x = to_slots(tokens)
    cot = to_slots(cotangent)
    gate_pre = lax.dot_general(x, w_gate[0], BY_FEATURE, preferred_element_type=jnp.float32)
    up_pre = lax.dot_general(x, w_up[0], BY_FEATURE, preferred_element_type=jnp.float32)
    sigma = jax.nn.sigmoid(gate_pre)
    hidden = gate_pre * sigma * up_pre
    scaled_hidden = (hidden * gate_slot).astype(jnp.bfloat16)

    y = jnp.dot(scaled_hidden, w_down[0], preferred_element_type=jnp.float32).astype(jnp.bfloat16)
    y = y.reshape(2, near, cap_rows, width)
    y = jnp.concatenate([y[0], swap(y[1], "expert", 1)], axis=1)
    y = jnp.einsum("gct,gcd->gtd", pick, y, preferred_element_type=jnp.float32)
    layer_out = hand_back(y.astype(jnp.bfloat16), own_rows)

    back = lax.dot_general(cot, w_down[0], BY_FEATURE, preferred_element_type=jnp.float32)
    slot_dot = jnp.sum(hidden * back, axis=1).reshape(2, near, cap_rows, 1)
    back = back * gate_slot
    grad_gate_pre = (back * up_pre * sigma * (1.0 + gate_pre * (1.0 - sigma))).astype(jnp.bfloat16)
    grad_up_pre = (back * gate_pre * sigma).astype(jnp.bfloat16)

    tok_dot = jnp.sum(jnp.where(own_pick, slot_dot, 0.0), axis=2)
    tok_dot = tok_dot.reshape(2, near, 2, dp_count, own_rows // 2).transpose(1, 0, 3, 2, 4)
    tok_dot = reorder(tok_dot).reshape(-1, 1)
    tok_dot = jnp.where(experts == me, tok_dot, 0.0)
    tok_dot = lax.psum_scatter(tok_dot, ("expert", "dp"), scatter_dimension=0, tiled=True)
    gate_grad = jnp.sum(jnp.where(share(named), tok_dot[:, None, :], 0.0), axis=2)

    grad_down = lax.dot_general(scaled_hidden, cot, BY_ROW, preferred_element_type=jnp.float32)
    grad_gate = lax.dot_general(grad_gate_pre, x, BY_ROW, preferred_element_type=jnp.float32)
    grad_up = lax.dot_general(grad_up_pre, x, BY_ROW, preferred_element_type=jnp.float32)
    return (
        layer_out,
        gate_grad,
        grad_gate.astype(jnp.bfloat16)[None],
        grad_up.astype(jnp.bfloat16)[None],
        grad_down.astype(jnp.bfloat16)[None],
    )


def solution(mesh):
    return jax.shard_map(
        body,
        mesh=mesh,
        in_specs=(
            P("expert", None),
            P("expert", None),
            P("expert", None),
            P("expert", None),
            P("expert", "dp", None),
            P("expert", "dp", None),
            P("expert", "dp", None),
        ),
        out_specs=(
            P(("expert", "dp"), None),
            P(("expert", "dp"), None),
            P("expert", "dp", None),
            P("expert", "dp", None),
            P("expert", "dp", None),
        ),
        check_vma=False,
    )
```

time: 733 us -> 528 us (0.72)
  waiting for transfers between devices: 431 us -> 220 us
  blocking collectives: 0 us -> 58 us
  starting transfers between devices: 88 us -> 38.4 us
  local copies, waits for them, and re-layouts: 52.2 us -> 35.7 us
  other arithmetic: 22.7 us -> 37.9 us
    all_to_all x3 -> x0, waiting for transfers between devices: 385 us -> none  [the longest x1 148 us: body(): lax.all_to_all(send_x, 'expert', split_axis=0, concat_axis=0, tiled=True)]
    ppermute x0 -> x24, waiting for transfers between devices: none -> 164 us  [swap(): return lax.ppermute(a, axis, [(i, i ^ bits) for i in range(size)])]
    all_to_all x3 -> x0, starting transfers between devices: 87.3 us -> none  [the longest x1 39.9 us: body(): lax.all_to_all(send_dy, 'expert', split_axis=0, concat_axis=0, tiled=True)]
    all_gather x0 -> x1, blocking collectives: none -> 58 us  [body(): gates = lax.all_gather(gates, 'expert', tiled=True)]
    ppermute x0 -> x24, starting transfers between devices: none -> 38.4 us  [swap(): return lax.ppermute(a, axis, [(i, i ^ bits) for i in range(size)])]
    gather x1 -> x0, local copies, waits for them, and re-layouts: 32.5 us -> none  [body(): y_slots = y_home[flat_ids, slot_rank].reshape(tok_rows, top_slots, width)]
    unnamed x3 -> x2, waiting for transfers between devices: 25 us -> 55.7 us
    concatenate x1 -> x8, other arithmetic: 0.02 us -> 24.1 us  [the longest x2 12.7 us: collect(): jnp.concatenate([along_y(along_dp(first)), along_dp(along_y(second))], ax...]
  transfers between devices with their start and end apart: 5 -> 25, of which waited for: 5 -> 9; matrix products, arithmetic and copies ran while one was open for 18% -> 25% of each run, Pallas kernels for 0% -> 0%
where the time goes in v1:
time: 528 us; the launch traced here: 525 us
  waiting for transfers between devices  220 us (42%)
  matrix products  120 us (23%)
  blocking collectives  58 us (11%)
  starting transfers between devices  38.4 us (7%)
  other arithmetic  37.9 us (7%)
  local copies, waits for them, and re-layouts  35.7 us (7%)
  between operations  14.9 us (3%)
    ppermute x24, waiting for transfers between devices, swap(): return lax.ppermute(a, axis, [(i, i ^ bits) for i in range(size)])  164 us
    all_gather x1, blocking collectives, body(): gates = lax.all_gather(gates, 'expert', tiled=True)  58 us
    unnamed x2, waiting for transfers between devices  55.7 us
    ppermute x24, starting transfers between devices, swap(): return lax.ppermute(a, axis, [(i, i ^ bits) for i in range(size)])  38.4 us
    dot_general x1, matrix products, body(): lax.dot_general(grad_gate_pre, x, BY_ROW, preferred_element_type=jnp.floa...  18 us
    dot_general x1, matrix products, body(): jnp.dot(scaled_hidden, w_down[0], preferred_element_type=jnp.float32)  16.7 us
    dot_general x1, matrix products, body(): lax.dot_general(scaled_hidden, cot, BY_ROW, preferred_element_type=jnp.fl...  15.7 us
    dot_general x1, matrix products, body(): lax.dot_general(grad_up_pre, x, BY_ROW, preferred_element_type=jnp.float32)  15.4 us
  transfers between devices with their start and end apart: 25, of which 9 were waited for; matrix products, arithmetic and copies ran while one was open for 25% of the time, Pallas kernels for 0%

profile of v1, /device:TPU:0, one launch (start us, length us, event | category | flops | bytes accessed | tf_op | source)
XLA Modules:
  0.0 524.8 jit_solution(5581564985974840924)
XLA Ops:
  7.2 1.9 constant_dynamic-slice_fusion
  9.1 4.0 collective-permute-start.17
  13.2 1.6 collective-permute-start.16
  14.7 0.8 constant_dynamic-slice_fusion.1
  16.0 3.9 collective-permute-start.2
  20.7 58.0 %all_gather.3 = f32[2048,16]{0,1:T(8,128)S(1)} all-gather(f32[128,16]{0,1:T(8,128)S(1)} %select_reduce_fusion.8), channel_id=1, replica_groups=mesh['dp'=2,'expert'=16] {'expert'}, dimensions={0}, use_global_device_ids=true | all-gather | bytes 139264 | tf_op jit(solution)/shard_map/all_gather | solution.py:71
  79.0 6.4 %collective-permute-start.18 = (bf16[64,3584]{1,0:T(8,128)(2,1)}, bf16[64,3584]{1,0:T(8,128)(2,1)S(1)}, u32[]{:S(2)}, u32[]{:S(2)}) collective-permute-start(bf16[64,3584]{1,0:T(8,128)(2,1)} %constant_dynamic-slice_fusion), channel_id=1, source_target_pairs={{0,12},{1,13},{2,14},{3,15},{4,8},{5,9},{6,10},{7,11},{8,4},{9,5},... | collective-permute-start | bytes 1376264 | tf_op jit(solution)/shard_map/ppermute | solution.py:12
  85.4 1.2 pad_maximum_fusion.2
  86.8 1.6 collective-permute-start.3
  88.4 2.7 collective-permute-start.5
  91.1 5.5 %collective-permute-done.18 = bf16[64,3584]{1,0:T(8,128)(2,1)S(1)} collective-permute-done((bf16[64,3584]{1,0:T(8,128)(2,1)}, bf16[64,3584]{1,0:T(8,128)(2,1)S(1)}, u32[]{:S(2)}, u32[]{:S(2)}) %collective-permute-start.18) | collective-permute-done | bytes 458784 | tf_op jit(solution)/shard_map/ppermute | solution.py:12
  96.6 1.2 pad_maximum_fusion.5
  97.8 11.2 %collective-permute-done.3 = bf16[4,1,1,1,32,3584]{5,4,0,3,2,1:T(8,128)(2,1)S(1)} collective-permute-done((bf16[4,1,1,1,32,3584]{5,4,0,3,2,1:T(8,128)(2,1)S(1)}, bf16[4,1,1,1,32,3584]{5,4,0,3,2,1:T(8,128)(2,1)S(1)}, u32[]{:S(2)}, u32[]{:S(2)}) %collective-permute-start.3) | collective-permute-done | bytes 917536 | tf_op jit(solution)/shard_map/ppermute | solution.py:12
  109.0 1.5 pad_maximum_fusion.3
  110.5 2.7 collective-permute-start.4
  113.3 1.5 pad_maximum_fusion.4
  114.8 1.5 collective-permute-start.6
  116.3 1.1 slice_bitcast_fusion.3
  118.7 56.9 %collective-permute-done.19 = bf16[4,1,1,1,32,3584]{5,4,0,3,2,1:T(8,128)(2,1)} collective-permute-done((bf16[4,1,1,1,32,3584]{5,4,0,3,2,1:T(8,128)(2,1)S(1)}, bf16[4,1,1,1,32,3584]{5,4,0,3,2,1:T(8,128)(2,1)}, u32[]{:S(2)}, u32[]{:S(2)}) %collective-permute-start.19) | collective-permute-done | bytes 917536 | tf_op jit(solution)/shard_map/ppermute | solution.py:12
  175.6 2.6 pad_maximum_fusion.6
  178.5 6.6 %maximum_maximum_fusion = bf16[4,2,2,2,32,3584]{5,4,0,3,2,1:T(8,128)(2,1)} fusion(bf16[4,2,1,1,32,3584]{5,4,0,3,2,1:T(8,128)(2,1)} %collective-permute-done.6, bf16[4,1,1,1,32,3584]{5,4,0,3,2,1:T(8,128)(2,1)} %copy-done.10, bf16[4,1,1,1,32,3584]{5,4,0,3,2,1:T(8,128)(2,1)S(1)} %get-tuple-element.19, ...), kind=kLoop, calls=%fused_computation.8 | loop fusion | flops 18350080 | bytes 14680064 | tf_op jit(solution)/shard_map/concatenate | solution.py:29
  185.1 3.8 copy.52
  189.0 3.9 convolution_convert_fusion.6
  193.3 1.0 copy-done.11
  194.3 1.4 pad_maximum_fusion.7
  195.7 1.5 collective-permute-start.22
  197.8 20.7 %collective-permute-done.20 = bf16[4,1,1,2,32,3584]{5,4,0,3,2,1:T(8,128)(2,1)} collective-permute-done((bf16[4,1,1,2,32,3584]{5,4,0,3,2,1:T(8,128)(2,1)}, bf16[4,1,1,2,32,3584]{5,4,0,3,2,1:T(8,128)(2,1)}, u32[]{:S(2)}, u32[]{:S(2)}) %collective-permute-start.20) | collective-permute-done | bytes 1835040 | tf_op jit(solution)/shard_map/ppermute | solution.py:12
  218.4 20.0 %collective-permute-done.22 = bf16[4,2,1,1,32,3584]{5,4,0,3,2,1:T(8,128)(2,1)} collective-permute-done((bf16[4,2,1,1,32,3584]{5,4,0,3,2,1:T(8,128)(2,1)}, bf16[4,2,1,1,32,3584]{5,4,0,3,2,1:T(8,128)(2,1)}, u32[]{:S(2)}, u32[]{:S(2)}) %collective-permute-start.22) | collective-permute-done | bytes 1835040 | tf_op jit(solution)/shard_map/ppermute | solution.py:12
  238.5 6.1 %maximum_maximum_fusion.1 = bf16[4,2,2,2,32,3584]{5,4,0,3,2,1:T(8,128)(2,1)} fusion(bf16[4,2,1,1,32,3584]{5,4,0,3,2,1:T(8,128)(2,1)} %collective-permute-done.22, bf16[4,1,1,1,32,3584]{5,4,0,3,2,1:T(8,128)(2,1)} %copy-done.11, bf16[4,1,1,1,32,3584]{5,4,0,3,2,1:T(8,128)(2,1)S(1)} %copy-done.8, bf16[4,1,1,2,32,3584]{5,4,0,3,2,1:T(8,128)(2,1)} %collective-permute-done.20, ...), kind=kLoop, calls=%fused_computation.9 | loop fusion | flops 18350080 | bytes 14680064 | tf_op jit(solution)/shard_map/concatenate | solution.py:29
  244.6 3.8 copy.55
  248.4 1.3 convolution_convert_fusion.4
  249.9 1.3 convolution_convert_fusion.5
  251.9 1.3 convolution_convert_fusion.7
  253.2 3.6 pad_maximum_fusion
  256.8 14.6 %fusion.12 = f32[1280,896]{0,1:T(8,128)} fusion(bf16[1280,3584]{1,0:T(8,128)(2,1)S(1)} %bitcast.93, bf16[1,896,3584]{2,1,0:T(8,128)(2,1)} %param.11), kind=kOutput, calls=%fused_computation.18 | convolution fusion | flops 8220835840 | bytes 20185088 | tf_op jit(solution)/shard_map/dot_general | solution.py:109
  271.4 10.1 %fusion.10 = f32[1280,896]{0,1:T(8,128)} fusion(bf16[1280,3584]{1,0:T(8,128)(2,1)S(1)} %bitcast.94, bf16[1,896,3584]{2,1,0:T(8,128)(2,1)S(1)} %bitcast.116), kind=kOutput, calls=%fused_computation.16 | convolution fusion | flops 8220835840 | bytes 20185088 | tf_op jit(solution)/shard_map/dot_general | solution.py:110
  281.5 0.9 pad_maximum_fusion.1
  282.4 2.6 copy-done.19
  284.9 14.2 %multiply_reduce_fusion = (f32[1280]{0:T(1024)S(1)}, f32[1280,896]{0,1:T(8,128)}) fusion(f32[1280,896]{0,1:T(8,128)} %fusion.10, f32[1280,896]{0,1:T(8,128)S(1)} %copy-done.19, bf16[1280,3584]{1,0:T(8,128)(2,1)S(1)} %bitcast.101, bf16[1,896,3584]{2,1,0:T(8,128)(2,1)} %param.13), kind=kOutput, calls=%fused_computation.29 | convolution fusion | flops 8228862976 | bytes 29365248 | tf_op jit(solution)/shard_map/dot_general | solution.py:121
  299.8 16.7 %convolution_convert_fusion = bf16[1280,3584]{1,0:T(8,128)(2,1)} fusion(bf16[1,896,3584]{2,1,0:T(8,128)(2,1)} %param.13, f32[1280]{0:T(1024)S(1)} %mul.60, f32[1280,896]{0,1:T(8,128)} %fusion.10, f32[1280,896]{0,1:T(8,128)} %fusion.12), kind=kOutput, calls=%fused_computation | convolution fusion | flops 8233451520 | bytes 24777728 | tf_op jit(solution)/shard_map/dot_general | solution.py:115
  316.5 7.9 %fusion.63 = (bf16[640,3584]{1,0:T(8,128)(2,1)}, bf16[640,3584]{1,0:T(8,128)(2,1)}) fusion(bf16[1280,3584]{1,0:T(8,128)(2,1)} %convolution_convert_fusion), kind=kLoop, calls=%fused_computation.131 | loop fusion | bytes 18350080 | tf_op jit(solution)/shard_map/slice | solution.py:117
  324.5 18.0 %fusion.14 = bf16[1,896,3584]{2,1,0:T(8,128)(2,1)} fusion(bf16[1280,3584]{1,0:T(8,128)(2,1)S(1)} %bitcast.97, f32[1280,896]{0,1:T(8,128)} %fusion.12, f32[1280,896]{0,1:T(8,128)} %fusion.10, f32[1280,896]{0,1:T(8,128)} %get-tuple-element.23, f32[1280]{0:T(1024)S(1)} %mul.60), kind=kOutput, calls=%fused_computation.24 | convolution fusion | flops 8236662784 | bytes 29365248 | tf_op jit(solution)/shard_map/dot_general | solution.py:135
  342.6 2.1 copy-done.18
  344.6 7.4 %fusion.4 = bf16[8,128,3584]{2,1,0:T(8,128)(2,1)} fusion(bf16[8,80,3584]{2,1,0:T(8,128)(2,1)} %copy-done.18, bf16[8,80,3584]{2,1,0:T(8,128)(2,1)} %bitcast.106, pred[8,80,128]{2,1,0:T(8,128)(4,1)S(1)} %iota_compare_fusion.1, pred[8,80,128]{2,1,0:T(8,128)(4,1)S(1)} %slice_bitcast_fusion.6), kind=kOutput, calls=%fused_computation.7 | convolution fusion | flops 1196589056 | bytes 16678912 | tf_op jit(solution)/shard_map/gct,gcd->gtd/dot_general | solution.py:118
  352.0 4.3 slice_bitcast_fusion.1
  356.5 1.6 slice.112
  358.1 1.5 collective-permute-start.11
  359.6 1.7 collective-permute-start.9
  361.3 15.7 %fusion.16 = bf16[1,896,3584]{2,1,0:T(8,128)(2,1)} fusion(bf16[1280,3584]{1,0:T(8,128)(2,1)S(1)} %bitcast.104, f32[1280]{0:T(1024)S(1)} %mul.60, f32[1280,896]{0,1:T(8,128)} %fusion.10, f32[1280,896]{0,1:T(8,128)} %fusion.12), kind=kOutput, calls=%fused_computation.26 | convolution fusion | flops 8232075264 | bytes 24777728 | tf_op jit(solution)/shard_map/dot_general | solution.py:134
  377.6 1.3 copy.57
  379.0 26.0 %collective-permute-done.11 = bf16[4,2,1,32,3584]{4,3,2,1,0:T(8,128)(2,1)} collective-permute-done((bf16[4,2,1,32,3584]{4,3,2,1,0:T(8,128)(2,1)}, bf16[4,2,1,32,3584]{4,3,2,1,0:T(8,128)(2,1)}, u32[]{:S(2)}, u32[]{:S(2)}) %collective-permute-start.11) | collective-permute-done | bytes 1835040 | tf_op jit(solution)/shard_map/ppermute | solution.py:12
  405.1 2.7 add_convert_fusion
  407.9 2.3 collective-permute-start.12
  410.2 2.0 add_convert_fusion.1
  412.3 1.9 collective-permute-start.10
  414.1 17.0 %collective-permute-done.12 = bf16[4,1,1,32,3584]{4,3,2,1,0:T(8,128)(2,1)S(1)} collective-permute-done((bf16[4,1,1,32,3584]{4,3,2,1,0:T(8,128)(2,1)S(1)}, bf16[4,1,1,32,3584]{4,3,2,1,0:T(8,128)(2,1)S(1)}, u32[]{:S(2)}, u32[]{:S(2)}) %collective-permute-start.12) | collective-permute-done | bytes 917536 | tf_op jit(solution)/shard_map/ppermute | solution.py:12
  431.4 6.4 %collective-permute-done.10 = bf16[4,1,1,32,3584]{4,3,2,1,0:T(8,128)(2,1)S(1)} collective-permute-done((bf16[4,1,1,32,3584]{4,3,2,1,0:T(8,128)(2,1)S(1)}, bf16[4,1,1,32,3584]{4,3,2,1,0:T(8,128)(2,1)S(1)}, u32[]{:S(2)}, u32[]{:S(2)}) %collective-permute-start.10) | collective-permute-done | bytes 917536 | tf_op jit(solution)/shard_map/ppermute | solution.py:12
  438.0 1.1 fusion.34
  439.2 1.8 collective-permute-start.13
  441.0 1.8 collective-permute-start.15
  442.8 15.4 %fusion.15 = bf16[1,896,3584]{2,1,0:T(8,128)(2,1)} fusion(bf16[1280,3584]{1,0:T(8,128)(2,1)S(1)} %bitcast.100, f32[1280,896]{0,1:T(8,128)} %fusion.12, f32[1280,896]{0,1:T(8,128)} %get-tuple-element.23, f32[1280]{0:T(1024)S(1)} %mul.60), kind=kOutput, calls=%fused_computation.25 | convolution fusion | flops 8232075264 | bytes 24777728 | tf_op jit(solution)/shard_map/dot_general | solution.py:136
  458.3 55.7 %reduce-scatter.4.cloned.1.call-done = f32[64,16]{1,0:T(8,128)} async-done(((f32[2048,16]{1,0:T(8,128)}), f32[64,16]{1,0:T(8,128)}) %reduce-scatter.4.cloned.1.call-update) | async-done | bytes 4112
  514.0 0.8 copy.58
  515.5 2.2 fusion.25
  (136 shorter events, 7.8 us)
Async XLA Ops:
  7.2 7.6 %copy-start = (bf16[128,3584]{1,0:T(8,128)(2,1)S(1)}, bf16[128,3584]{1,0:T(8,128)(2,1)}, u32[]{:S(2)}) copy-start(bf16[128,3584]{1,0:T(8,128)(2,1)} %param.7) | copy-start | bytes 2752516
  7.2 506.8 %reduce-scatter.4.cloned.1.call-start = ((), (), s32[]{:S(2)}) async-start(), calls=%async_computation.1 | async-start | bytes 1081344
  9.1 79.2 %copy-start.12 = (bf16[128,3584]{1,0:T(8,128)(2,1)S(1)}, bf16[128,3584]{1,0:T(8,128)(2,1)}, u32[]{:S(2)}) copy-start(bf16[128,3584]{1,0:T(8,128)(2,1)} %param.8) | copy-start | bytes 2752516
  9.1 81.9 %collective-permute-start.17 = (bf16[64,3584]{1,0:T(8,128)(2,1)}, bf16[64,3584]{1,0:T(8,128)(2,1)S(1)}, u32[]{:S(2)}, u32[]{:S(2)}) collective-permute-start(bf16[64,3584]{1,0:T(8,128)(2,1)} %constant_dynamic-slice_fusion), channel_id=1, source_target_pairs={{0,8},{1,9},{2,10},{3,11},{4,12},{5,13},{6,14},{7,15},{8,0},{9,1},... | collective-permute-start | bytes 1376264 | tf_op jit(solution)/shard_map/ppermute | solution.py:12
  13.2 77.9 %collective-permute-start.16 = (bf16[64,3584]{1,0:T(8,128)(2,1)}, bf16[64,3584]{1,0:T(8,128)(2,1)}, u32[]{:S(2)}, u32[]{:S(2)}) collective-permute-start(bf16[64,3584]{1,0:T(8,128)(2,1)} %constant_dynamic-slice_fusion), channel_id=1, source_target_pairs={{0,4},{1,5},{2,6},{3,7},{4,0},{5,1},{6,2},{7,3},{8,12},{9,13},{10,... | collective-permute-start | bytes 1376264 | tf_op jit(solution)/shard_map/ppermute | solution.py:12
  15.5 63.4 %collective-permute-start.1 = (bf16[64,3584]{1,0:T(8,128)(2,1)}, bf16[64,3584]{1,0:T(8,128)(2,1)S(1)}, u32[]{:S(2)}, u32[]{:S(2)}) collective-permute-start(bf16[64,3584]{1,0:T(8,128)(2,1)} %constant_dynamic-slice_fusion.1), channel_id=1, source_target_pairs={{0,8},{1,9},{2,10},{3,11},{4,12},{5,13},{6,14},{7,15},{8,0},{9,1},... | collective-permute-start | bytes 1376264 | tf_op jit(solution)/shard_map/ppermute | solution.py:12
  15.9 69.5 %collective-permute-start = (bf16[64,3584]{1,0:T(8,128)(2,1)}, bf16[64,3584]{1,0:T(8,128)(2,1)S(1)}, u32[]{:S(2)}, u32[]{:S(2)}) collective-permute-start(bf16[64,3584]{1,0:T(8,128)(2,1)} %constant_dynamic-slice_fusion.1), channel_id=1, source_target_pairs={{0,4},{1,5},{2,6},{3,7},{4,0},{5,1},{6,2},{7,3},{8,12},{9,13},{10,... | collective-permute-start | bytes 1376264 | tf_op jit(solution)/shard_map/ppermute | solution.py:12
  16.0 69.4 %collective-permute-start.2 = (bf16[64,3584]{1,0:T(8,128)(2,1)}, bf16[64,3584]{1,0:T(8,128)(2,1)}, u32[]{:S(2)}, u32[]{:S(2)}) collective-permute-start(bf16[64,3584]{1,0:T(8,128)(2,1)} %constant_dynamic-slice_fusion.1), channel_id=1, source_target_pairs={{0,12},{1,13},{2,14},{3,15},{4,8},{5,9},{6,10},{7,11},{8,4},{9,5},... | collective-permute-start | bytes 1376264 | tf_op jit(solution)/shard_map/ppermute | solution.py:12
  19.9 58.9 %copy-start.16 = (pred[16]{0:T(512)(128)(4,1)}, pred[16]{0:T(512)(128)(4,1)S(1)}, u32[]{:S(2)}) copy-start(pred[16]{0:T(512)(128)(4,1)S(1)} %get-tuple-element.25) | copy-start | bytes 52
  79.0 17.6 %collective-permute-start.18 = (bf16[64,3584]{1,0:T(8,128)(2,1)}, bf16[64,3584]{1,0:T(8,128)(2,1)S(1)}, u32[]{:S(2)}, u32[]{:S(2)}) collective-permute-start(bf16[64,3584]{1,0:T(8,128)(2,1)} %constant_dynamic-slice_fusion), channel_id=1, source_target_pairs={{0,12},{1,13},{2,14},{3,15},{4,8},{5,9},{6,10},{7,11},{8,4},{9,5},... | collective-permute-start | bytes 1376264 | tf_op jit(solution)/shard_map/ppermute | solution.py:12
  86.8 22.3 %collective-permute-start.3 = (bf16[4,1,1,1,32,3584]{5,4,0,3,2,1:T(8,128)(2,1)S(1)}, bf16[4,1,1,1,32,3584]{5,4,0,3,2,1:T(8,128)(2,1)S(1)}, u32[]{:S(2)}, u32[]{:S(2)}) collective-permute-start(bf16[4,1,1,1,32,3584]{5,4,0,3,2,1:T(8,128)(2,1)S(1)} %get-tuple-element.18), channel_id=1, source_target_pairs={{0,16},{16,0},{1,17},{17,1},{2,18},{18,2},{3,19},{19,3},{4,20},{20... | collective-permute-start | bytes 2752520 | tf_op jit(solution)/shard_map/ppermute | solution.py:12
  88.4 24.9 %collective-permute-start.5 = (bf16[4,1,1,1,32,3584]{5,4,0,3,2,1:T(8,128)(2,1)S(1)}, bf16[4,1,1,1,32,3584]{5,4,0,3,2,1:T(8,128)(2,1)S(1)}, u32[]{:S(2)}, u32[]{:S(2)}) collective-permute-start(bf16[4,1,1,1,32,3584]{5,4,0,3,2,1:T(8,128)(2,1)S(1)} %get-tuple-element.19), channel_id=1, source_target_pairs={{0,2},{1,3},{2,0},{3,1},{4,6},{5,7},{6,4},{7,5},{8,10},{9,11},{10,... | collective-permute-start | bytes 2752520 | tf_op jit(solution)/shard_map/ppermute | solution.py:12
  109.0 8.3 %copy-start.9 = (bf16[4,1,1,1,32,3584]{5,4,0,3,2,1:T(8,128)(2,1)}, bf16[4,1,1,1,32,3584]{5,4,0,3,2,1:T(8,128)(2,1)S(1)}, u32[]{:S(2)}) copy-start(bf16[4,1,1,1,32,3584]{5,4,0,3,2,1:T(8,128)(2,1)S(1)} %collective-permute-done.3) | copy-start | bytes 2752516
  110.5 68.0 %collective-permute-start.4 = (bf16[4,1,1,2,32,3584]{5,4,0,3,2,1:T(8,128)(2,1)}, bf16[4,1,1,2,32,3584]{5,4,0,3,2,1:T(8,128)(2,1)}, u32[]{:S(2)}, u32[]{:S(2)}) collective-permute-start(bf16[4,1,1,2,32,3584]{5,4,0,3,2,1:T(8,128)(2,1)} %pad_maximum_fusion.3), channel_id=1, source_target_pairs={{0,2},{1,3},{2,0},{3,1},{4,6},{5,7},{6,4},{7,5},{8,10},{9,11},{10,... | collective-permute-start | bytes 5505032 | tf_op jit(solution)/shard_map/ppermute | solution.py:12
  113.3 4.1 copy-start.10
  114.8 63.7 %collective-permute-start.6 = (bf16[4,2,1,1,32,3584]{5,4,0,3,2,1:T(8,128)(2,1)}, bf16[4,2,1,1,32,3584]{5,4,0,3,2,1:T(8,128)(2,1)}, u32[]{:S(2)}, u32[]{:S(2)}) collective-permute-start(bf16[4,2,1,1,32,3584]{5,4,0,3,2,1:T(8,128)(2,1)} %pad_maximum_fusion.4), channel_id=1, source_target_pairs={{0,16},{16,0},{1,17},{17,1},{2,18},{18,2},{3,19},{19,3},{4,20},{20... | collective-permute-start | bytes 5505032 | tf_op jit(solution)/shard_map/ppermute | solution.py:12
  117.4 58.3 %collective-permute-start.19 = (bf16[4,1,1,1,32,3584]{5,4,0,3,2,1:T(8,128)(2,1)S(1)}, bf16[4,1,1,1,32,3584]{5,4,0,3,2,1:T(8,128)(2,1)}, u32[]{:S(2)}, u32[]{:S(2)}) collective-permute-start(bf16[4,1,1,1,32,3584]{5,4,0,3,2,1:T(8,128)(2,1)S(1)} %get-tuple-element.20), channel_id=1, source_target_pairs={{0,16},{16,0},{1,17},{17,1},{2,18},{18,2},{3,19},{19,3},{4,20},{20... | collective-permute-start | bytes 2752520 | tf_op jit(solution)/shard_map/ppermute | solution.py:12
  118.0 67.2 %copy-start.13 = (pred[32,32]{1,0:T(8,128)(4,1)}, pred[32,32]{1,0:T(8,128)(4,1)S(1)}, u32[]{:S(2)}) copy-start(pred[32,32]{1,0:T(8,128)(4,1)S(1)} %iota_compare_fusion.6) | copy-start | bytes 3076
  118.7 74.6 %collective-permute-start.21 = (bf16[4,1,1,1,32,3584]{5,4,0,3,2,1:T(8,128)(2,1)}, bf16[4,1,1,1,32,3584]{5,4,0,3,2,1:T(8,128)(2,1)S(1)}, u32[]{:S(2)}, u32[]{:S(2)}) collective-permute-start(bf16[4,1,1,1,32,3584]{5,4,0,3,2,1:T(8,128)(2,1)} %get-tuple-element.21), channel_id=1, source_target_pairs={{0,2},{1,3},{2,0},{3,1},{4,6},{5,7},{6,4},{7,5},{8,10},{9,11},{10,... | collective-permute-start | bytes 2752520 | tf_op jit(solution)/shard_map/ppermute | solution.py:12
  178.2 40.3 %collective-permute-start.20 = (bf16[4,1,1,2,32,3584]{5,4,0,3,2,1:T(8,128)(2,1)}, bf16[4,1,1,2,32,3584]{5,4,0,3,2,1:T(8,128)(2,1)}, u32[]{:S(2)}, u32[]{:S(2)}) collective-permute-start(bf16[4,1,1,2,32,3584]{5,4,0,3,2,1:T(8,128)(2,1)} %pad_maximum_fusion.6), channel_id=1, source_target_pairs={{0,2},{1,3},{2,0},{3,1},{4,6},{5,7},{6,4},{7,5},{8,10},{9,11},{10,... | collective-permute-start | bytes 5505032 | tf_op jit(solution)/shard_map/ppermute | solution.py:12
  189.0 4.3 copy-start.2
  189.0 5.3 %copy-start.8 = (bf16[4,1,1,1,32,3584]{5,4,0,3,2,1:T(8,128)(2,1)S(1)}, bf16[4,1,1,1,32,3584]{5,4,0,3,2,1:T(8,128)(2,1)}, u32[]{:S(2)}) copy-start(bf16[4,1,1,1,32,3584]{5,4,0,3,2,1:T(8,128)(2,1)} %get-tuple-element.21) | copy-start | bytes 2752516
  193.3 59.9 %collective-permute-start.7 = (bf16[8,80,3584]{2,1,0:T(8,128)(2,1)}, bf16[8,80,3584]{2,1,0:T(8,128)(2,1)}, u32[]{:S(2)}, u32[]{:S(2)}) collective-permute-start(bf16[8,80,3584]{2,1,0:T(8,128)(2,1)} %convolution_convert_fusion.6), channel_id=1, source_target_pairs={{0,1},{1,0},{2,3},{3,2},{4,5},{5,4},{6,7},{7,6},{8,9},{9,8},{10,11... | collective-permute-start | bytes 13762568 | tf_op jit(solution)/shard_map/ppermute | solution.py:12
  193.3 1.0 copy-start.11
  195.7 42.7 %collective-permute-start.22 = (bf16[4,2,1,1,32,3584]{5,4,0,3,2,1:T(8,128)(2,1)}, bf16[4,2,1,1,32,3584]{5,4,0,3,2,1:T(8,128)(2,1)}, u32[]{:S(2)}, u32[]{:S(2)}) collective-permute-start(bf16[4,2,1,1,32,3584]{5,4,0,3,2,1:T(8,128)(2,1)} %pad_maximum_fusion.7), channel_id=1, source_target_pairs={{0,16},{16,0},{1,17},{17,1},{2,18},{18,2},{3,19},{19,3},{4,20},{20... | collective-permute-start | bytes 5505032 | tf_op jit(solution)/shard_map/ppermute | solution.py:12
  248.4 2.8 slice-start
  249.8 2.1 slice-start.1
  249.8 31.7 %collective-permute-start.23 = (bf16[8,80,3584]{2,1,0:T(8,128)(2,1)S(1)}, bf16[8,80,3584]{2,1,0:T(8,128)(2,1)S(1)}, u32[]{:S(2)}, u32[]{:S(2)}) collective-permute-start(bf16[8,80,3584]{2,1,0:T(8,128)(2,1)S(1)} %convolution_convert_fusion.4), channel_id=1, source_target_pairs={{0,1},{1,0},{2,3},{3,2},{4,5},{5,4},{6,7},{7,6},{8,9},{9,8},{10,11... | collective-permute-start | bytes 13762568 | tf_op jit(solution)/shard_map/ppermute | solution.py:12
  253.2 18.2 %slice-start.11 = ((s8[6422528]{0:T(1024)(128)(4,1)}), s8[2228224]{0:T(1024)(128)(4,1)S(1)}, s32[]{:S(2)}) async-start(s8[6422528]{0:T(1024)(128)(4,1)} %bitcast.115), calls=%async_computation.13 | async-start | bytes 4456448
  256.8 14.6 %copy-start.6 = (bf16[16,80,3584]{2,1,0:T(8,128)(2,1)}, bf16[16,80,3584]{2,1,0:T(8,128)(2,1)S(1)}, u32[]{:S(2)}) copy-start(bf16[16,80,3584]{2,1,0:T(8,128)(2,1)S(1)} %pad_maximum_fusion) | copy-start | bytes 27525124
  256.8 14.6 %slice-start.12 = ((s8[6422528]{0:T(1024)(128)(4,1)}), s8[4194304]{0:T(1024)(128)(4,1)S(1)}, s32[]{:S(2)}) async-start(s8[6422528]{0:T(1024)(128)(4,1)} %bitcast.115), calls=%async_computation.14 | async-start | bytes 8388608
  281.5 3.5 copy-start.19
  282.4 16.7 %copy-start.7 = (bf16[16,80,3584]{2,1,0:T(8,128)(2,1)}, bf16[16,80,3584]{2,1,0:T(8,128)(2,1)S(1)}, u32[]{:S(2)}) copy-start(bf16[16,80,3584]{2,1,0:T(8,128)(2,1)S(1)} %pad_maximum_fusion.1) | copy-start | bytes 27525124
  299.8 24.7 %slice-start.2 = ((s8[9175040]{0:T(1024)(128)(4,1)}), s8[4194304]{0:T(1024)(128)(4,1)S(1)}, s32[]{:S(2)}) async-start(s8[9175040]{0:T(1024)(128)(4,1)} %bitcast.95), calls=%async_computation.4 | async-start | bytes 8388608
  299.8 24.7 %slice-start.3 = ((s8[9175040]{0:T(1024)(128)(4,1)}), s8[4194304]{0:T(1024)(128)(4,1)S(1)}, s32[]{:S(2)}) async-start(s8[9175040]{0:T(1024)(128)(4,1)} %bitcast.95), calls=%async_computation.5 | async-start | bytes 8388608
  316.5 7.9 %copy-start.15 = (s32[128,8]{0,1:T(8,128)S(1)}, s32[128,8]{0,1:T(8,128)}, u32[]{:S(2)}) copy-start(s32[128,8]{0,1:T(8,128)} %param.9) | copy-start | bytes 12292
  316.5 8.0 %slice-start.4 = ((s8[9175040]{0:T(1024)(128)(4,1)}), s8[786432]{0:T(1024)(128)(4,1)S(1)}, s32[]{:S(2)}) async-start(s8[9175040]{0:T(1024)(128)(4,1)} %bitcast.95), calls=%async_computation.6 | async-start | bytes 1572864
  324.4 18.2 %collective-permute-start.8 = (bf16[8,80,3584]{2,1,0:T(8,128)(2,1)}, bf16[8,80,3584]{2,1,0:T(8,128)(2,1)S(1)}, u32[]{:S(2)}, u32[]{:S(2)}) collective-permute-start(bf16[8,80,3584]{2,1,0:T(8,128)(2,1)} %bitcast.107), channel_id=1, source_target_pairs={{0,1},{1,0},{2,3},{3,2},{4,5},{5,4},{6,7},{7,6},{8,9},{9,8},{10,11... | collective-permute-start | bytes 13762568 | tf_op jit(solution)/shard_map/ppermute | solution.py:12
  342.6 2.1 copy-start.18
  344.6 16.7 %slice-start.8 = ((s8[9175040]{0:T(1024)(128)(4,1)}), s8[4194304]{0:T(1024)(128)(4,1)S(1)}, s32[]{:S(2)}) async-start(s8[9175040]{0:T(1024)(128)(4,1)} %bitcast.102), calls=%async_computation.10 | async-start | bytes 8388608
  344.6 16.7 %slice-start.9 = ((s8[9175040]{0:T(1024)(128)(4,1)}), s8[4194304]{0:T(1024)(128)(4,1)S(1)}, s32[]{:S(2)}) async-start(s8[9175040]{0:T(1024)(128)(4,1)} %bitcast.102), calls=%async_computation.11 | async-start | bytes 8388608
  352.0 9.3 %slice-start.10 = ((s8[9175040]{0:T(1024)(128)(4,1)}), s8[786432]{0:T(1024)(128)(4,1)S(1)}, s32[]{:S(2)}) async-start(s8[9175040]{0:T(1024)(128)(4,1)} %bitcast.102), calls=%async_computation.12 | async-start | bytes 1572864
  356.4 20.7 %copy-start.3 = (bf16[4,2,2,32,3584]{4,3,2,1,0:T(8,128)(2,1)}, bf16[4,2,2,32,3584]{4,3,2,1,0:T(8,128)(2,1)S(1)}, u32[]{:S(2)}) copy-start(bf16[4,2,2,32,3584]{4,3,2,1,0:T(8,128)(2,1)S(1)} %get-tuple-element.13) | copy-start | bytes 11010052
  356.4 20.7 %copy-start.5 = (bf16[4,2,2,32,3584]{4,3,2,1,0:T(8,128)(2,1)}, bf16[4,2,2,32,3584]{4,3,2,1,0:T(8,128)(2,1)S(1)}, u32[]{:S(2)}) copy-start(bf16[4,2,2,32,3584]{4,3,2,1,0:T(8,128)(2,1)S(1)} %get-tuple-element.14) | copy-start | bytes 11010052
  358.1 19.1 %copy-start.14 = (pred[32,32]{1,0:T(8,128)(4,1)S(1)}, pred[32,32]{1,0:T(8,128)(4,1)}, u32[]{:S(2)}) copy-start(pred[32,32]{1,0:T(8,128)(4,1)} %copy-done.13) | copy-start | bytes 3076
  358.1 19.4 %copy-start.17 = (pred[16]{0:T(512)(128)(4,1)S(1)}, pred[16]{0:T(512)(128)(4,1)}, u32[]{:S(2)}) copy-start(pred[16]{0:T(512)(128)(4,1)} %copy-done.16) | copy-start | bytes 52
  358.1 47.0 %collective-permute-start.11 = (bf16[4,2,1,32,3584]{4,3,2,1,0:T(8,128)(2,1)}, bf16[4,2,1,32,3584]{4,3,2,1,0:T(8,128)(2,1)}, u32[]{:S(2)}, u32[]{:S(2)}) collective-permute-start(bf16[4,2,1,32,3584]{4,3,2,1,0:T(8,128)(2,1)} %slice.112), channel_id=1, source_target_pairs={{0,16},{16,0},{1,17},{17,1},{2,18},{18,2},{3,19},{19,3},{4,20},{20... | collective-permute-start | bytes 5505032 | tf_op jit(solution)/shard_map/ppermute | solution.py:12
  359.6 50.6 %collective-permute-start.9 = (bf16[4,1,2,32,3584]{4,3,2,1,0:T(8,128)(2,1)S(1)}, bf16[4,1,2,32,3584]{4,3,2,1,0:T(8,128)(2,1)}, u32[]{:S(2)}, u32[]{:S(2)}) collective-permute-start(bf16[4,1,2,32,3584]{4,3,2,1,0:T(8,128)(2,1)S(1)} %slice.107), channel_id=1, source_target_pairs={{0,2},{1,3},{2,0},{3,1},{4,6},{5,7},{6,4},{7,5},{8,10},{9,11},{10,... | collective-permute-start | bytes 5505032 | tf_op jit(solution)/shard_map/ppermute | solution.py:12
  379.0 31.2 %copy-start.4 = (bf16[4,2,2,32,3584]{4,3,2,1,0:T(8,128)(2,1)S(1)}, bf16[4,2,2,32,3584]{4,3,2,1,0:T(8,128)(2,1)}, u32[]{:S(2)}) copy-start(bf16[4,2,2,32,3584]{4,3,2,1,0:T(8,128)(2,1)} %copy-done.3) | copy-start | bytes 11010052
  405.1 37.7 %slice-start.5 = ((s8[9175040]{0:T(1024)(128)(4,1)}), s8[4194304]{0:T(1024)(128)(4,1)S(1)}, s32[]{:S(2)}) async-start(s8[9175040]{0:T(1024)(128)(4,1)} %bitcast.98), calls=%async_computation.7 | async-start | bytes 8388608
  407.9 34.9 %slice-start.6 = ((s8[9175040]{0:T(1024)(128)(4,1)}), s8[4194304]{0:T(1024)(128)(4,1)S(1)}, s32[]{:S(2)}) async-start(s8[9175040]{0:T(1024)(128)(4,1)} %bitcast.98), calls=%async_computation.8 | async-start | bytes 8388608
  407.9 23.3 %collective-permute-start.12 = (bf16[4,1,1,32,3584]{4,3,2,1,0:T(8,128)(2,1)S(1)}, bf16[4,1,1,32,3584]{4,3,2,1,0:T(8,128)(2,1)S(1)}, u32[]{:S(2)}, u32[]{:S(2)}) collective-permute-start(bf16[4,1,1,32,3584]{4,3,2,1,0:T(8,128)(2,1)S(1)} %slice.114), channel_id=1, source_target_pairs={{0,2},{1,3},{2,0},{3,1},{4,6},{5,7},{6,4},{7,5},{8,10},{9,11},{10,... | collective-permute-start | bytes 2752520 | tf_op jit(solution)/shard_map/ppermute | solution.py:12
  412.3 30.6 %slice-start.7 = ((s8[9175040]{0:T(1024)(128)(4,1)}), s8[786432]{0:T(1024)(128)(4,1)S(1)}, s32[]{:S(2)}) async-start(s8[9175040]{0:T(1024)(128)(4,1)} %bitcast.98), calls=%async_computation.9 | async-start | bytes 1572864
  412.3 25.6 %collective-permute-start.10 = (bf16[4,1,1,32,3584]{4,3,2,1,0:T(8,128)(2,1)S(1)}, bf16[4,1,1,32,3584]{4,3,2,1,0:T(8,128)(2,1)S(1)}, u32[]{:S(2)}, u32[]{:S(2)}) collective-permute-start(bf16[4,1,1,32,3584]{4,3,2,1,0:T(8,128)(2,1)S(1)} %slice.109), channel_id=1, source_target_pairs={{0,16},{16,0},{1,17},{17,1},{2,18},{18,2},{3,19},{19,3},{4,20},{20... | collective-permute-start | bytes 2752520 | tf_op jit(solution)/shard_map/ppermute | solution.py:12
  439.2 76.3 %collective-permute-start.13 = (bf16[64,3584]{1,0:T(8,128)(2,1)}, bf16[64,3584]{1,0:T(8,128)(2,1)S(1)}, u32[]{:S(2)}, u32[]{:S(2)}) collective-permute-start(bf16[64,3584]{1,0:T(8,128)(2,1)} %get-tuple-element.15), channel_id=1, source_target_pairs={{0,4},{1,5},{2,6},{3,7},{4,0},{5,1},{6,2},{7,3},{8,12},{9,13},{10,... | collective-permute-start | bytes 1376264 | tf_op jit(solution)/shard_map/ppermute | solution.py:12
  441.0 74.5 %collective-permute-start.15 = (bf16[64,3584]{1,0:T(8,128)(2,1)}, bf16[64,3584]{1,0:T(8,128)(2,1)}, u32[]{:S(2)}, u32[]{:S(2)}) collective-permute-start(bf16[64,3584]{1,0:T(8,128)(2,1)} %get-tuple-element.16), channel_id=1, source_target_pairs={{0,12},{1,13},{2,14},{3,15},{4,8},{5,9},{6,10},{7,11},{8,4},{9,5},... | collective-permute-start | bytes 1376264 | tf_op jit(solution)/shard_map/ppermute | solution.py:12
  442.8 72.7 %collective-permute-start.14 = (bf16[64,3584]{1,0:T(8,128)(2,1)}, bf16[64,3584]{1,0:T(8,128)(2,1)}, u32[]{:S(2)}, u32[]{:S(2)}) collective-permute-start(bf16[64,3584]{1,0:T(8,128)(2,1)} %get-tuple-element.17), channel_id=1, source_target_pairs={{0,8},{1,9},{2,10},{3,11},{4,12},{5,13},{6,14},{7,15},{8,0},{9,1},... | collective-permute-start | bytes 1376264 | tf_op jit(solution)/shard_map/ppermute | solution.py:12
  442.8 74.8 %copy-start.1 = (bf16[128,3584]{1,0:T(8,128)(2,1)S(1)}, bf16[128,3584]{1,0:T(8,128)(2,1)}, u32[]{:S(2)}) copy-start(bf16[128,3584]{1,0:T(8,128)(2,1)} %param.7) | copy-start | bytes 2752516
Sparse Core Ops, SparseCore 0:
  379.1 134.7 reduce-scatter.3

commit v2 on v1

--- a/solution.py
+++ b/solution.py
@@ -12,10 +12,12 @@
     return lax.ppermute(a, axis, [(i, i ^ bits) for i in range(size)])
 
 
-def collect(a):
+def collect(a, after=None):
     dp_count = lax.axis_size("dp")
     z_count = lax.axis_size("expert") // 4
     rows, width = a.shape
+    if after is not None:
+        a, _ = lax.optimization_barrier((a, after))
     a = jnp.stack([a] + [swap(a, "expert", 4 * z) for z in range(1, z_count)])
     first = a[:, None, None, None, : rows // 2]
     second = a[:, None, None, None, rows // 2 :]
@@ -27,7 +29,7 @@
         return jnp.concatenate([b] + [swap(b, "dp", d) for d in range(1, dp_count)], axis=3)
 
     both = jnp.concatenate([along_y(along_dp(first)), along_dp(along_y(second))], axis=2)
-    return both.reshape(2 * z_count, dp_count * rows, width)
+    return both.reshape(2 * z_count, dp_count * rows, width), a
 
 
 def hand_back(a, rows):
@@ -68,7 +70,9 @@
     experts = jnp.arange(groups, dtype=jnp.int32)
     named = route_ids[:, :, None] == experts[None, None, :]
     gates = jnp.sum(jnp.where(named, route_gates[:, :, None], 0.0), axis=1)
-    gates = lax.all_gather(gates, "expert", tiled=True)
+    gates = gates.T
+    gates = jnp.stack([gates, gates[experts ^ 1]], axis=1)
+    gates = lax.all_to_all(gates, "expert", split_axis=0, concat_axis=0, tiled=True)
 
     block = jnp.arange(groups * dp_count, dtype=jnp.int32)
     partner = (block // dp_count ^ me) * dp_count + (block % dp_count ^ part)
@@ -77,8 +81,7 @@
     def reorder(a):
         return jnp.sum(jnp.where(partner, a.reshape(1, -1, own_rows), 0.0), axis=1)
 
-    def near_far(expert):
-        a = jnp.sum(jnp.where(experts == expert, gates, 0.0), axis=1)
+    def near_far(a):
         a = reorder(a).reshape(near, 2, dp_count, 2, own_rows // 2)
         return a.transpose(1, 0, 3, 2, 4).reshape(2, near, tok_rows)
 
@@ -91,21 +94,22 @@
         rank = jnp.where(chosen, count - 1.0, -1.0)
         return rank[..., None, :] == places[:, None]
 
-    own_gates = near_far(me)
+    own_gates = near_far(gates[:, 0])
     own_pick = slots(own_gates)
     gate_slot = jnp.sum(jnp.where(own_pick, own_gates[:, :, None, :], 0.0), axis=3).reshape(-1, 1)
-    pair_pick = slots(near_far(me ^ 1)[0])
+    pair_pick = slots(near_far(gates[:, 1])[0])
     pick = jnp.concatenate([own_pick[0], pair_pick], axis=1).astype(jnp.bfloat16)
 
     def to_slots(a):
-        a = collect(share(a))
         rows = jnp.einsum("gct,gtd->gcd", pick[:, cap_rows:], a, preferred_element_type=jnp.float32)
         sent = swap(rows.astype(jnp.bfloat16), "expert", 1)
         rows = jnp.einsum("gct,gtd->gcd", pick[:, :cap_rows], a, preferred_element_type=jnp.float32)
         return jnp.concatenate([rows.astype(jnp.bfloat16), sent]).reshape(-1, width)
 
-    x = to_slots(tokens)
-    cot = to_slots(cotangent)
+    all_x, column = collect(share(tokens), gates)
+    all_cot, _ = collect(share(cotangent), column)
+    x = to_slots(all_x)
+    cot = to_slots(all_cot)
     gate_pre = lax.dot_general(x, w_gate[0], BY_FEATURE, preferred_element_type=jnp.float32)
     up_pre = lax.dot_general(x, w_up[0], BY_FEATURE, preferred_element_type=jnp.float32)
     sigma = jax.nn.sigmoid(gate_pre)
@@ -126,10 +130,10 @@
 
     tok_dot = jnp.sum(jnp.where(own_pick, slot_dot, 0.0), axis=2)
     tok_dot = tok_dot.reshape(2, near, 2, dp_count, own_rows // 2).transpose(1, 0, 3, 2, 4)
-    tok_dot = reorder(tok_dot).reshape(-1, 1)
-    tok_dot = jnp.where(experts == me, tok_dot, 0.0)
-    tok_dot = lax.psum_scatter(tok_dot, ("expert", "dp"), scatter_dimension=0, tiled=True)
-    gate_grad = jnp.sum(jnp.where(share(named), tok_dot[:, None, :], 0.0), axis=2)
+    tok_dot = reorder(tok_dot)
+    tok_dot = lax.all_to_all(tok_dot, ("expert", "dp"), split_axis=0, concat_axis=0, tiled=True)
+    tok_dot = jnp.sum(tok_dot.reshape(groups, dp_count, own_rows), axis=1)
+    gate_grad = jnp.sum(jnp.where(share(named), tok_dot.T[:, None, :], 0.0), axis=2)
 
     grad_down = lax.dot_general(scaled_hidden, cot, BY_ROW, preferred_element_type=jnp.float32)
     grad_gate = lax.dot_general(grad_gate_pre, x, BY_ROW, preferred_element_type=jnp.float32)

time: 528 us -> 429 us (0.81); the launches traced: 525 us -> 420 us
  blocking collectives: 58 us -> 0 us
  waiting for transfers between devices: 220 us -> 194 us
  between operations: 14.9 us -> 1.7 us
  local copies, waits for them, and re-layouts: 35.7 us -> 24.4 us
    all_gather x1 -> x0, blocking collectives: 58 us -> none  [body(): gates = lax.all_gather(gates, 'expert', tiled=True)]
    unnamed x2 -> x0, waiting for transfers between devices: 55.7 us -> none
    ppermute x24, waiting for transfers between devices: 164 us -> 187 us  [swap(): return lax.ppermute(a, axis, [(i, i ^ bits) for i in range(size)])]
    ppermute x24, starting transfers between devices: 38.4 us -> 26.4 us  [swap(): return lax.ppermute(a, axis, [(i, i ^ bits) for i in range(size)])]
    all_to_all x0 -> x2, starting transfers between devices: none -> 10.1 us  [the longest x1 7.39 us: body(): lax.all_to_all(gates, 'expert', split_axis=0, concat_axis=0, tiled=True)]
    unnamed x68 -> x62, local copies, waits for them, and re-layouts: 8.96 us -> 0.51 us
    all_to_all x0 -> x2, waiting for transfers between devices: none -> 6.43 us  [the longest x1 6.43 us: body(): lax.all_to_all(gates, 'expert', split_axis=0, concat_axis=0, tiled=True)]
  transfers between devices with their start and end apart: 25 -> 26, of which waited for: 9 -> 15; matrix products, arithmetic and copies ran while one was open for 25% -> 30% of each run, Pallas kernels for 0% -> 0%
where the time goes in v2:
time: 429 us; the launch traced here: 420 us
  waiting for transfers between devices  194 us (45%)
  matrix products  123 us (29%)
  other arithmetic  41.2 us (10%)
  starting transfers between devices  36.5 us (9%)
  local copies, waits for them, and re-layouts  24.4 us (6%)
    ppermute x24, waiting for transfers between devices, swap(): return lax.ppermute(a, axis, [(i, i ^ bits) for i in range(size)])  187 us
    ppermute x24, starting transfers between devices, swap(): return lax.ppermute(a, axis, [(i, i ^ bits) for i in range(size)])  26.4 us
    dot_general x1, matrix products, body(): lax.dot_general(grad_gate_pre, x, BY_ROW, preferred_element_type=jnp.floa...  17.9 us
    dot_general x1, matrix products, body(): jnp.dot(scaled_hidden, w_down[0], preferred_element_type=jnp.float32)  16.7 us
    dot_general x1, matrix products, body(): lax.dot_general(scaled_hidden, cot, BY_ROW, preferred_element_type=jnp.fl...  15.5 us
    dot_general x1, matrix products, body(): lax.dot_general(grad_up_pre, x, BY_ROW, preferred_element_type=jnp.float32)  15.4 us
    dot_general x1, matrix products, body(): lax.dot_general(cot, w_down[0], BY_FEATURE, preferred_element_type=jnp.fl...  14.9 us
    dot_general x1, matrix products, body(): lax.dot_general(x, w_gate[0], BY_FEATURE, preferred_element_type=jnp.floa...  14 us
  transfers between devices with their start and end apart: 26, of which 15 were waited for; matrix products, arithmetic and copies ran while one was open for 30% of the time, Pallas kernels for 0%

profile of v2, /device:TPU:0, one launch (start us, length us, event | category | flops | bytes accessed | tf_op | source)
XLA Modules:
  0.0 420.4 jit_solution(17071716703918262406)
XLA Ops:
  0.7 0.8 select_reduce_fusion.6
  2.7 7.4 %all-to-all-start = ((f32[16,2,128]{2,1,0:T(2,128)}), f32[16,2,128]{2,1,0:T(2,128)S(1)}, u32[]{:S(2)}, u32[]{:S(2)}) async-start(f32[16,2,128]{2,1,0:T(2,128)} %copy.65), calls=%async_computation | async-start | bytes 32768 | tf_op jit(solution)/shard_map/all_to_all | solution.py:75
  10.1 6.4 %all-to-all-done = f32[16,2,128]{2,1,0:T(2,128)S(1)} async-done(((f32[16,2,128]{2,1,0:T(2,128)}), f32[16,2,128]{2,1,0:T(2,128)S(1)}, u32[]{:S(2)}, u32[]{:S(2)}) %all-to-all-start) | async-done | bytes 16416 | tf_op jit(solution)/shard_map/all_to_all | solution.py:75
  17.1 1.4 collective-permute-start.1
  18.5 2.5 collective-permute-start
  20.9 10.9 %collective-permute-done.2 = bf16[64,3584]{1,0:T(8,128)(2,1)S(1)} collective-permute-done((bf16[64,3584]{1,0:T(8,128)(2,1)S(1)}, bf16[64,3584]{1,0:T(8,128)(2,1)S(1)}, u32[]{:S(2)}, u32[]{:S(2)}) %collective-permute-start.2) | collective-permute-done | bytes 458784 | tf_op jit(solution)/shard_map/ppermute | solution.py:12
  31.9 26.6 %collective-permute-done.1 = bf16[64,3584]{1,0:T(8,128)(2,1)S(1)} collective-permute-done((bf16[64,3584]{1,0:T(8,128)(2,1)S(1)}, bf16[64,3584]{1,0:T(8,128)(2,1)S(1)}, u32[]{:S(2)}, u32[]{:S(2)}) %collective-permute-start.1) | collective-permute-done | bytes 458784 | tf_op jit(solution)/shard_map/ppermute | solution.py:12
  58.9 1.6 collective-permute-start.3
  60.4 0.7 collective-permute-start.5
  61.8 1.6 collective-permute-start.18
  63.3 2.9 collective-permute-start.16
  66.2 14.2 %collective-permute-done.3 = bf16[4,1,1,1,32,3584]{5,4,0,3,2,1:T(8,128)(2,1)S(1)} collective-permute-done((bf16[4,1,1,1,32,3584]{5,4,0,3,2,1:T(8,128)(2,1)S(1)}, bf16[4,1,1,1,32,3584]{5,4,0,3,2,1:T(8,128)(2,1)S(1)}, u32[]{:S(2)}, u32[]{:S(2)}) %collective-permute-start.3) | collective-permute-done | bytes 917536 | tf_op jit(solution)/shard_map/ppermute | solution.py:12
  80.5 1.5 pad_maximum_fusion.3
  82.5 2.6 pad_maximum_fusion.4
  85.1 1.5 collective-permute-start.6
  86.9 13.7 %collective-permute-done.17 = bf16[64,3584]{1,0:T(8,128)(2,1)} collective-permute-done((bf16[64,3584]{1,0:T(8,128)(2,1)S(1)}, bf16[64,3584]{1,0:T(8,128)(2,1)}, u32[]{:S(2)}, u32[]{:S(2)}) %collective-permute-start.17) | collective-permute-done | bytes 458784 | tf_op jit(solution)/shard_map/ppermute | solution.py:12
  100.7 1.5 pad_maximum_fusion.5
  103.0 1.4 collective-permute-start.21
  104.4 20.8 %collective-permute-done.4 = bf16[4,1,1,2,32,3584]{5,4,0,3,2,1:T(8,128)(2,1)} collective-permute-done((bf16[4,1,1,2,32,3584]{5,4,0,3,2,1:T(8,128)(2,1)}, bf16[4,1,1,2,32,3584]{5,4,0,3,2,1:T(8,128)(2,1)}, u32[]{:S(2)}, u32[]{:S(2)}) %collective-permute-start.4) | collective-permute-done | bytes 1835040 | tf_op jit(solution)/shard_map/ppermute | solution.py:12
  125.2 3.2 collective-permute-done.6
  128.4 6.1 %maximum_maximum_fusion = bf16[4,2,2,2,32,3584]{5,4,0,3,2,1:T(8,128)(2,1)} fusion(bf16[4,2,1,1,32,3584]{5,4,0,3,2,1:T(8,128)(2,1)} %collective-permute-done.6, bf16[4,1,1,1,32,3584]{5,4,0,3,2,1:T(8,128)(2,1)} %collective-permute-done.5, bf16[4,1,1,1,32,3584]{5,4,0,3,2,1:T(8,128)(2,1)S(1)} %get-tuple-element.23, ...), kind=kLoop, calls=%fused_computation.9 | loop fusion | flops 18350080 | bytes 14680064 | tf_op jit(solution)/shard_map/concatenate | solution.py:31
  134.5 3.8 copy.69
  138.4 3.9 convolution_convert_fusion.6
  142.7 2.4 collective-permute-done.19
  145.1 1.5 pad_maximum_fusion.6
  146.6 1.4 collective-permute-start.20
  148.0 2.6 pad_maximum_fusion.7
  150.6 1.5 collective-permute-start.22
  152.6 4.6 %convolution_convert_fusion.7 = bf16[8,80,3584]{2,1,0:T(8,128)(2,1)S(1)} fusion(bf16[8,128,3584]{2,1,0:T(8,128)(2,1)} %bitcast.96, pred[2,8,80,128]{3,2,1,0:T(8,128)(4,1)S(1)} %iota_compare_fusion), kind=kOutput, calls=%fused_computation.24 | convolution fusion | flops 589496320 | bytes 12009472 | tf_op jit(solution)/shard_map/gct,gtd->gcd/dot_general | solution.py:106
  157.2 29.7 %collective-permute-done.20 = bf16[4,1,1,2,32,3584]{5,4,0,3,2,1:T(8,128)(2,1)} collective-permute-done((bf16[4,1,1,2,32,3584]{5,4,0,3,2,1:T(8,128)(2,1)}, bf16[4,1,1,2,32,3584]{5,4,0,3,2,1:T(8,128)(2,1)}, u32[]{:S(2)}, u32[]{:S(2)}) %collective-permute-start.20) | collective-permute-done | bytes 1835040 | tf_op jit(solution)/shard_map/ppermute | solution.py:12
  186.9 3.7 collective-permute-done.22
  190.7 5.9 %maximum_maximum_fusion.1 = bf16[4,2,2,2,32,3584]{5,4,0,3,2,1:T(8,128)(2,1)} fusion(bf16[4,2,1,1,32,3584]{5,4,0,3,2,1:T(8,128)(2,1)} %collective-permute-done.22, bf16[4,1,1,1,32,3584]{5,4,0,3,2,1:T(8,128)(2,1)} %collective-permute-done.21, bf16[4,1,1,1,32,3584]{5,4,0,3,2,1:T(8,128)(2,1)S(1)} %copy-done.9, ...), kind=kLoop, calls=%fused_computation.10 | loop fusion | flops 18350080 | bytes 14680064 | tf_op jit(solution)/shard_map/concatenate | solution.py:31
  196.6 3.8 copy.72
  200.4 1.3 convolution_convert_fusion.4
  201.8 1.3 convolution_convert_fusion.5
  203.2 3.6 pad_maximum_fusion
  206.8 14.0 %fusion.12 = f32[1280,896]{0,1:T(8,128)S(1)} fusion(bf16[1280,3584]{1,0:T(8,128)(2,1)S(1)} %bitcast.99, bf16[1,896,3584]{2,1,0:T(8,128)(2,1)} %param.11), kind=kOutput, calls=%fused_computation.19 | convolution fusion | flops 8220835840 | bytes 20185088 | tf_op jit(solution)/shard_map/dot_general | solution.py:113
  220.9 10.1 %fusion.10 = f32[1280,896]{0,1:T(8,128)} fusion(bf16[1280,3584]{1,0:T(8,128)(2,1)S(1)} %bitcast.100, bf16[1,896,3584]{2,1,0:T(8,128)(2,1)S(1)} %bitcast.128), kind=kOutput, calls=%fused_computation.17 | convolution fusion | flops 8220835840 | bytes 20185088 | tf_op jit(solution)/shard_map/dot_general | solution.py:114
  230.9 3.7 pad_maximum_fusion.1
  234.7 14.9 %multiply_reduce_fusion = (f32[1280]{0:T(1024)S(1)}, f32[1280,896]{0,1:T(8,128)}) fusion(f32[1280,896]{0,1:T(8,128)S(1)} %copy-done.19, f32[1280,896]{0,1:T(8,128)S(1)} %fusion.12, bf16[1280,3584]{1,0:T(8,128)(2,1)S(1)} %bitcast.107, bf16[1,896,3584]{2,1,0:T(8,128)(2,1)} %param.13), kind=kOutput, calls=%fused_computation.30 | convolution fusion | flops 8228862976 | bytes 29365248 | tf_op jit(solution)/shard_map/dot_general | solution.py:125
  250.3 16.7 %convolution_convert_fusion = bf16[1280,3584]{1,0:T(8,128)(2,1)} fusion(bf16[1,896,3584]{2,1,0:T(8,128)(2,1)} %param.13, f32[1280]{0:T(1024)S(1)} %mul.60, f32[1280,896]{0,1:T(8,128)} %fusion.10, f32[1280,896]{0,1:T(8,128)} %copy-done.18), kind=kOutput, calls=%fused_computation.1 | convolution fusion | flops 8233451520 | bytes 24777728 | tf_op jit(solution)/shard_map/dot_general | solution.py:119
  267.0 8.0 %fusion.64 = (bf16[640,3584]{1,0:T(8,128)(2,1)}, bf16[640,3584]{1,0:T(8,128)(2,1)}) fusion(bf16[1280,3584]{1,0:T(8,128)(2,1)} %convolution_convert_fusion), kind=kLoop, calls=%fused_computation.133 | loop fusion | bytes 18350080 | tf_op jit(solution)/shard_map/slice | solution.py:121
  275.7 17.9 %fusion.14 = bf16[1,896,3584]{2,1,0:T(8,128)(2,1)} fusion(bf16[1280,3584]{1,0:T(8,128)(2,1)S(1)} %bitcast.103, f32[1280,896]{0,1:T(8,128)} %copy-done.18, f32[1280,896]{0,1:T(8,128)} %fusion.10, f32[1280,896]{0,1:T(8,128)} %get-tuple-element.27, f32[1280]{0:T(1024)S(1)} %mul.60), kind=kOutput, calls=%fused_computation.25 | convolution fusion | flops 8236662784 | bytes 29365248 | tf_op jit(solution)/shard_map/dot_general | solution.py:139
  293.6 6.6 %fusion.4 = bf16[8,128,3584]{2,1,0:T(8,128)(2,1)} fusion(bf16[8,80,3584]{2,1,0:T(8,128)(2,1)} %collective-permute-done.8, bf16[8,80,3584]{2,1,0:T(8,128)(2,1)S(1)} %bitcast.112, pred[8,80,128]{2,1,0:T(8,128)(4,1)S(1)} %iota_compare_fusion.1, pred[8,80,128]{2,1,0:T(8,128)(4,1)S(1)} %slice_bitcast_fusion.6), kind=kOutput, calls=%fused_computation.8 | convolution fusion | flops 1196589056 | bytes 16678912 | tf_op jit(solution)/shard_map/gct,gcd->gtd/dot_general | solution.py:122
  300.3 4.0 slice_bitcast_fusion.1
  304.4 1.5 slice.124
  306.0 1.5 collective-permute-start.11
  308.1 15.5 %fusion.16 = bf16[1,896,3584]{2,1,0:T(8,128)(2,1)} fusion(bf16[1280,3584]{1,0:T(8,128)(2,1)S(1)} %bitcast.110, f32[1280]{0:T(1024)S(1)} %mul.60, f32[1280,896]{0,1:T(8,128)} %fusion.10, f32[1280,896]{0,1:T(8,128)} %copy-done.18), kind=kOutput, calls=%fused_computation.27 | convolution fusion | flops 8232075264 | bytes 24777728 | tf_op jit(solution)/shard_map/dot_general | solution.py:138
  323.8 0.8 select_reduce_fusion.2
  324.6 2.7 all-to-all-start.1
  327.3 21.1 %collective-permute-done.11 = bf16[4,2,1,32,3584]{4,3,2,1,0:T(8,128)(2,1)} collective-permute-done((bf16[4,2,1,32,3584]{4,3,2,1,0:T(8,128)(2,1)}, bf16[4,2,1,32,3584]{4,3,2,1,0:T(8,128)(2,1)}, u32[]{:S(2)}, u32[]{:S(2)}) %collective-permute-start.11) | collective-permute-done | bytes 1835040 | tf_op jit(solution)/shard_map/ppermute | solution.py:12
  348.4 2.7 add_convert_fusion
  351.8 2.2 add_convert_fusion.1
  354.2 1.6 collective-permute-start.10
  355.7 16.9 %collective-permute-done.12 = bf16[4,1,1,32,3584]{4,3,2,1,0:T(8,128)(2,1)S(1)} collective-permute-done((bf16[4,1,1,32,3584]{4,3,2,1,0:T(8,128)(2,1)S(1)}, bf16[4,1,1,32,3584]{4,3,2,1,0:T(8,128)(2,1)S(1)}, u32[]{:S(2)}, u32[]{:S(2)}) %collective-permute-start.12) | collective-permute-done | bytes 917536 | tf_op jit(solution)/shard_map/ppermute | solution.py:12
  372.9 2.3 collective-permute-done.10
  375.4 1.1 fusion.34
  376.6 1.5 collective-permute-start.15
  378.1 2.0 collective-permute-start.14
  380.1 15.4 %fusion.15 = bf16[1,896,3584]{2,1,0:T(8,128)(2,1)} fusion(bf16[1280,3584]{1,0:T(8,128)(2,1)S(1)} %bitcast.106, f32[1280,896]{0,1:T(8,128)} %copy-done.18, f32[1280,896]{0,1:T(8,128)} %get-tuple-element.27, f32[1280]{0:T(1024)S(1)} %mul.60), kind=kOutput, calls=%fused_computation.26 | convolution fusion | flops 8232075264 | bytes 24777728 | tf_op jit(solution)/shard_map/dot_general | solution.py:140
  395.5 0.7 select_reduce_fusion.5
  396.2 3.5 collective-permute-done.15
  399.8 18.0 %collective-permute-done.14 = bf16[64,3584]{1,0:T(8,128)(2,1)} collective-permute-done((bf16[64,3584]{1,0:T(8,128)(2,1)}, bf16[64,3584]{1,0:T(8,128)(2,1)}, u32[]{:S(2)}, u32[]{:S(2)}) %collective-permute-start.14) | collective-permute-done | bytes 458784 | tf_op jit(solution)/shard_map/ppermute | solution.py:12
  417.8 2.1 fusion.25
  (130 shorter events, 8.9 us)
Async XLA Ops:
  0.6 9.4 %copy-start = (bf16[128,3584]{1,0:T(8,128)(2,1)S(1)}, bf16[128,3584]{1,0:T(8,128)(2,1)}, u32[]{:S(2)}) copy-start(bf16[128,3584]{1,0:T(8,128)(2,1)} %param.7) | copy-start | bytes 2752516
  2.7 13.9 %all-to-all-start = ((f32[16,2,128]{2,1,0:T(2,128)}), f32[16,2,128]{2,1,0:T(2,128)S(1)}, u32[]{:S(2)}, u32[]{:S(2)}) async-start(f32[16,2,128]{2,1,0:T(2,128)} %copy.65), calls=%async_computation | async-start | bytes 32768 | tf_op jit(solution)/shard_map/all_to_all | solution.py:75
  16.5 15.3 %collective-permute-start.2 = (bf16[64,3584]{1,0:T(8,128)(2,1)S(1)}, bf16[64,3584]{1,0:T(8,128)(2,1)S(1)}, u32[]{:S(2)}, u32[]{:S(2)}) collective-permute-start(bf16[64,3584]{1,0:T(8,128)(2,1)S(1)} %constant_dynamic-slice_fusion.1), channel_id=1, source_target_pairs={{0,12},{1,13},{2,14},{3,15},{4,8},{5,9},{6,10},{7,11},{8,4},{9,5},... | collective-permute-start | bytes 1376264 | tf_op jit(solution)/shard_map/ppermute | solution.py:12
  17.1 41.4 %collective-permute-start.1 = (bf16[64,3584]{1,0:T(8,128)(2,1)S(1)}, bf16[64,3584]{1,0:T(8,128)(2,1)S(1)}, u32[]{:S(2)}, u32[]{:S(2)}) collective-permute-start(bf16[64,3584]{1,0:T(8,128)(2,1)S(1)} %constant_dynamic-slice_fusion.1), channel_id=1, source_target_pairs={{0,8},{1,9},{2,10},{3,11},{4,12},{5,13},{6,14},{7,15},{8,0},{9,1},... | collective-permute-start | bytes 1376264 | tf_op jit(solution)/shard_map/ppermute | solution.py:12
  18.5 40.0 %collective-permute-start = (bf16[64,3584]{1,0:T(8,128)(2,1)S(1)}, bf16[64,3584]{1,0:T(8,128)(2,1)S(1)}, u32[]{:S(2)}, u32[]{:S(2)}) collective-permute-start(bf16[64,3584]{1,0:T(8,128)(2,1)S(1)} %constant_dynamic-slice_fusion.1), channel_id=1, source_target_pairs={{0,4},{1,5},{2,6},{3,7},{4,0},{5,1},{6,2},{7,3},{8,12},{9,13},{10,... | collective-permute-start | bytes 1376264 | tf_op jit(solution)/shard_map/ppermute | solution.py:12
  20.9 39.5 %copy-start.14 = (bf16[128,3584]{1,0:T(8,128)(2,1)S(1)}, bf16[128,3584]{1,0:T(8,128)(2,1)}, u32[]{:S(2)}) copy-start(bf16[128,3584]{1,0:T(8,128)(2,1)} %param.8) | copy-start | bytes 2752516
  58.9 21.6 %collective-permute-start.3 = (bf16[4,1,1,1,32,3584]{5,4,0,3,2,1:T(8,128)(2,1)S(1)}, bf16[4,1,1,1,32,3584]{5,4,0,3,2,1:T(8,128)(2,1)S(1)}, u32[]{:S(2)}, u32[]{:S(2)}) collective-permute-start(bf16[4,1,1,1,32,3584]{5,4,0,3,2,1:T(8,128)(2,1)S(1)} %get-tuple-element.22), channel_id=1, source_target_pairs={{0,16},{16,0},{1,17},{17,1},{2,18},{18,2},{3,19},{19,3},{4,20},{20... | collective-permute-start | bytes 2752520 | tf_op jit(solution)/shard_map/ppermute | solution.py:12
  60.4 22.1 %collective-permute-start.5 = (bf16[4,1,1,1,32,3584]{5,4,0,3,2,1:T(8,128)(2,1)S(1)}, bf16[4,1,1,1,32,3584]{5,4,0,3,2,1:T(8,128)(2,1)}, u32[]{:S(2)}, u32[]{:S(2)}) collective-permute-start(bf16[4,1,1,1,32,3584]{5,4,0,3,2,1:T(8,128)(2,1)S(1)} %get-tuple-element.23), channel_id=1, source_target_pairs={{0,2},{1,3},{2,0},{3,1},{4,6},{5,7},{6,4},{7,5},{8,10},{9,11},{10,... | collective-permute-start | bytes 2752520 | tf_op jit(solution)/shard_map/ppermute | solution.py:12
  61.2 41.0 %copy-start.15 = (pred[32,32]{1,0:T(8,128)(4,1)}, pred[32,32]{1,0:T(8,128)(4,1)S(1)}, u32[]{:S(2)}) copy-start(pred[32,32]{1,0:T(8,128)(4,1)S(1)} %iota_compare_fusion.6) | copy-start | bytes 3076
  61.8 25.2 %collective-permute-start.18 = (bf16[64,3584]{1,0:T(8,128)(2,1)S(1)}, bf16[64,3584]{1,0:T(8,128)(2,1)}, u32[]{:S(2)}, u32[]{:S(2)}) collective-permute-start(bf16[64,3584]{1,0:T(8,128)(2,1)S(1)} %constant_dynamic-slice_fusion), channel_id=1, source_target_pairs={{0,12},{1,13},{2,14},{3,15},{4,8},{5,9},{6,10},{7,11},{8,4},{9,5},... | collective-permute-start | bytes 1376264 | tf_op jit(solution)/shard_map/ppermute | solution.py:12
  63.3 37.4 %collective-permute-start.17 = (bf16[64,3584]{1,0:T(8,128)(2,1)S(1)}, bf16[64,3584]{1,0:T(8,128)(2,1)}, u32[]{:S(2)}, u32[]{:S(2)}) collective-permute-start(bf16[64,3584]{1,0:T(8,128)(2,1)S(1)} %constant_dynamic-slice_fusion), channel_id=1, source_target_pairs={{0,8},{1,9},{2,10},{3,11},{4,12},{5,13},{6,14},{7,15},{8,0},{9,1},... | collective-permute-start | bytes 1376264 | tf_op jit(solution)/shard_map/ppermute | solution.py:12
  63.3 37.4 %collective-permute-start.16 = (bf16[64,3584]{1,0:T(8,128)(2,1)S(1)}, bf16[64,3584]{1,0:T(8,128)(2,1)}, u32[]{:S(2)}, u32[]{:S(2)}) collective-permute-start(bf16[64,3584]{1,0:T(8,128)(2,1)S(1)} %constant_dynamic-slice_fusion), channel_id=1, source_target_pairs={{0,4},{1,5},{2,6},{3,7},{4,0},{5,1},{6,2},{7,3},{8,12},{9,13},{10,... | collective-permute-start | bytes 1376264 | tf_op jit(solution)/shard_map/ppermute | solution.py:12
  80.5 20.2 %copy-start.11 = (bf16[4,1,1,1,32,3584]{5,4,0,3,2,1:T(8,128)(2,1)}, bf16[4,1,1,1,32,3584]{5,4,0,3,2,1:T(8,128)(2,1)S(1)}, u32[]{:S(2)}) copy-start(bf16[4,1,1,1,32,3584]{5,4,0,3,2,1:T(8,128)(2,1)S(1)} %collective-permute-done.3) | copy-start | bytes 2752516
  81.9 43.3 %collective-permute-start.4 = (bf16[4,1,1,2,32,3584]{5,4,0,3,2,1:T(8,128)(2,1)}, bf16[4,1,1,2,32,3584]{5,4,0,3,2,1:T(8,128)(2,1)}, u32[]{:S(2)}, u32[]{:S(2)}) collective-permute-start(bf16[4,1,1,2,32,3584]{5,4,0,3,2,1:T(8,128)(2,1)} %pad_maximum_fusion.3), channel_id=1, source_target_pairs={{0,2},{1,3},{2,0},{3,1},{4,6},{5,7},{6,4},{7,5},{8,10},{9,11},{10,... | collective-permute-start | bytes 5505032 | tf_op jit(solution)/shard_map/ppermute | solution.py:12
  85.1 43.3 %collective-permute-start.6 = (bf16[4,2,1,1,32,3584]{5,4,0,3,2,1:T(8,128)(2,1)}, bf16[4,2,1,1,32,3584]{5,4,0,3,2,1:T(8,128)(2,1)}, u32[]{:S(2)}, u32[]{:S(2)}) collective-permute-start(bf16[4,2,1,1,32,3584]{5,4,0,3,2,1:T(8,128)(2,1)} %pad_maximum_fusion.4), channel_id=1, source_target_pairs={{0,16},{16,0},{1,17},{17,1},{2,18},{18,2},{3,19},{19,3},{4,20},{20... | collective-permute-start | bytes 5505032 | tf_op jit(solution)/shard_map/ppermute | solution.py:12
  102.4 45.7 %copy-start.8 = (bf16[4,1,1,1,32,3584]{5,4,0,3,2,1:T(8,128)(2,1)}, bf16[4,1,1,1,32,3584]{5,4,0,3,2,1:T(8,128)(2,1)S(1)}, u32[]{:S(2)}) copy-start(bf16[4,1,1,1,32,3584]{5,4,0,3,2,1:T(8,128)(2,1)S(1)} %get-tuple-element.25) | copy-start | bytes 2752516
  102.4 42.7 %collective-permute-start.19 = (bf16[4,1,1,1,32,3584]{5,4,0,3,2,1:T(8,128)(2,1)S(1)}, bf16[4,1,1,1,32,3584]{5,4,0,3,2,1:T(8,128)(2,1)S(1)}, u32[]{:S(2)}, u32[]{:S(2)}) collective-permute-start(bf16[4,1,1,1,32,3584]{5,4,0,3,2,1:T(8,128)(2,1)S(1)} %get-tuple-element.24), channel_id=1, source_target_pairs={{0,16},{16,0},{1,17},{17,1},{2,18},{18,2},{3,19},{19,3},{4,20},{20... | collective-permute-start | bytes 2752520 | tf_op jit(solution)/shard_map/ppermute | solution.py:12
  103.0 45.1 %collective-permute-start.21 = (bf16[4,1,1,1,32,3584]{5,4,0,3,2,1:T(8,128)(2,1)S(1)}, bf16[4,1,1,1,32,3584]{5,4,0,3,2,1:T(8,128)(2,1)}, u32[]{:S(2)}, u32[]{:S(2)}) collective-permute-start(bf16[4,1,1,1,32,3584]{5,4,0,3,2,1:T(8,128)(2,1)S(1)} %get-tuple-element.25), channel_id=1, source_target_pairs={{0,2},{1,3},{2,0},{3,1},{4,6},{5,7},{6,4},{7,5},{8,10},{9,11},{10,... | collective-permute-start | bytes 2752520 | tf_op jit(solution)/shard_map/ppermute | solution.py:12
  138.4 4.3 %copy-start.2 = (bf16[4,2,2,2,32,3584]{5,4,3,2,1,0:T(8,128)(2,1)}, bf16[4,2,2,2,32,3584]{5,4,3,2,1,0:T(8,128)(2,1)S(1)}, u32[]{:S(2)}) copy-start(bf16[4,2,2,2,32,3584]{5,4,3,2,1,0:T(8,128)(2,1)S(1)} %copy.69) | copy-start | bytes 22020100
  142.7 60.5 %collective-permute-start.7 = (bf16[8,80,3584]{2,1,0:T(8,128)(2,1)}, bf16[8,80,3584]{2,1,0:T(8,128)(2,1)}, u32[]{:S(2)}, u32[]{:S(2)}) collective-permute-start(bf16[8,80,3584]{2,1,0:T(8,128)(2,1)} %convolution_convert_fusion.6), channel_id=1, source_target_pairs={{0,1},{1,0},{2,3},{3,2},{4,5},{5,4},{6,7},{7,6},{8,9},{9,8},{10,11... | collective-permute-start | bytes 13762568 | tf_op jit(solution)/shard_map/ppermute | solution.py:12
  145.1 5.5 %copy-start.12 = (bf16[4,1,1,1,32,3584]{5,4,0,3,2,1:T(8,128)(2,1)}, bf16[4,1,1,1,32,3584]{5,4,0,3,2,1:T(8,128)(2,1)S(1)}, u32[]{:S(2)}) copy-start(bf16[4,1,1,1,32,3584]{5,4,0,3,2,1:T(8,128)(2,1)S(1)} %collective-permute-done.19) | copy-start | bytes 2752516
  146.6 40.3 %collective-permute-start.20 = (bf16[4,1,1,2,32,3584]{5,4,0,3,2,1:T(8,128)(2,1)}, bf16[4,1,1,2,32,3584]{5,4,0,3,2,1:T(8,128)(2,1)}, u32[]{:S(2)}, u32[]{:S(2)}) collective-permute-start(bf16[4,1,1,2,32,3584]{5,4,0,3,2,1:T(8,128)(2,1)} %pad_maximum_fusion.6), channel_id=1, source_target_pairs={{0,2},{1,3},{2,0},{3,1},{4,6},{5,7},{6,4},{7,5},{8,10},{9,11},{10,... | collective-permute-start | bytes 5505032 | tf_op jit(solution)/shard_map/ppermute | solution.py:12
  150.6 40.0 %collective-permute-start.22 = (bf16[4,2,1,1,32,3584]{5,4,0,3,2,1:T(8,128)(2,1)}, bf16[4,2,1,1,32,3584]{5,4,0,3,2,1:T(8,128)(2,1)}, u32[]{:S(2)}, u32[]{:S(2)}) collective-permute-start(bf16[4,2,1,1,32,3584]{5,4,0,3,2,1:T(8,128)(2,1)} %pad_maximum_fusion.7), channel_id=1, source_target_pairs={{0,16},{16,0},{1,17},{17,1},{2,18},{18,2},{3,19},{19,3},{4,20},{20... | collective-permute-start | bytes 5505032 | tf_op jit(solution)/shard_map/ppermute | solution.py:12
  152.6 38.0 %copy-start.9 = (bf16[4,1,1,1,32,3584]{5,4,0,3,2,1:T(8,128)(2,1)S(1)}, bf16[4,1,1,1,32,3584]{5,4,0,3,2,1:T(8,128)(2,1)}, u32[]{:S(2)}) copy-start(bf16[4,1,1,1,32,3584]{5,4,0,3,2,1:T(8,128)(2,1)} %copy-done.8) | copy-start | bytes 2752516
  152.6 38.0 %copy-start.13 = (bf16[4,1,1,1,32,3584]{5,4,0,3,2,1:T(8,128)(2,1)S(1)}, bf16[4,1,1,1,32,3584]{5,4,0,3,2,1:T(8,128)(2,1)}, u32[]{:S(2)}) copy-start(bf16[4,1,1,1,32,3584]{5,4,0,3,2,1:T(8,128)(2,1)} %copy-done.12) | copy-start | bytes 2752516
  201.8 29.2 %collective-permute-start.23 = (bf16[8,80,3584]{2,1,0:T(8,128)(2,1)S(1)}, bf16[8,80,3584]{2,1,0:T(8,128)(2,1)}, u32[]{:S(2)}, u32[]{:S(2)}) collective-permute-start(bf16[8,80,3584]{2,1,0:T(8,128)(2,1)S(1)} %convolution_convert_fusion.4), channel_id=1, source_target_pairs={{0,1},{1,0},{2,3},{3,2},{4,5},{5,4},{6,7},{7,6},{8,9},{9,8},{10,11... | collective-permute-start | bytes 13762568 | tf_op jit(solution)/shard_map/ppermute | solution.py:12
  203.2 17.6 %slice-start.9 = ((s8[6422528]{0:T(1024)(128)(4,1)}), s8[2228224]{0:T(1024)(128)(4,1)S(1)}, s32[]{:S(2)}) async-start(s8[6422528]{0:T(1024)(128)(4,1)} %bitcast.127), calls=%async_computation.11 | async-start | bytes 4456448
  206.8 14.0 %copy-start.6 = (bf16[16,80,3584]{2,1,0:T(8,128)(2,1)}, bf16[16,80,3584]{2,1,0:T(8,128)(2,1)S(1)}, u32[]{:S(2)}) copy-start(bf16[16,80,3584]{2,1,0:T(8,128)(2,1)S(1)} %pad_maximum_fusion) | copy-start | bytes 27525124
  206.8 14.1 %slice-start.10 = ((s8[6422528]{0:T(1024)(128)(4,1)}), s8[4194304]{0:T(1024)(128)(4,1)S(1)}, s32[]{:S(2)}) async-start(s8[6422528]{0:T(1024)(128)(4,1)} %bitcast.127), calls=%async_computation.12 | async-start | bytes 8388608
  220.8 13.8 %copy-start.18 = (f32[1280,896]{0,1:T(8,128)}, f32[1280,896]{0,1:T(8,128)S(1)}, u32[]{:S(2)}) copy-start(f32[1280,896]{0,1:T(8,128)S(1)} %fusion.12) | copy-start | bytes 13762564
  230.9 3.8 copy-start.19
  234.7 14.9 %copy-start.7 = (bf16[16,80,3584]{2,1,0:T(8,128)(2,1)}, bf16[16,80,3584]{2,1,0:T(8,128)(2,1)S(1)}, u32[]{:S(2)}) copy-start(bf16[16,80,3584]{2,1,0:T(8,128)(2,1)S(1)} %pad_maximum_fusion.1) | copy-start | bytes 27525124
  250.3 25.3 %slice-start = ((s8[9175040]{0:T(1024)(128)(4,1)}), s8[4194304]{0:T(1024)(128)(4,1)S(1)}, s32[]{:S(2)}) async-start(s8[9175040]{0:T(1024)(128)(4,1)} %bitcast.101), calls=%async_computation.2 | async-start | bytes 8388608
  250.3 25.4 %slice-start.1 = ((s8[9175040]{0:T(1024)(128)(4,1)}), s8[4194304]{0:T(1024)(128)(4,1)S(1)}, s32[]{:S(2)}) async-start(s8[9175040]{0:T(1024)(128)(4,1)} %bitcast.101), calls=%async_computation.3 | async-start | bytes 8388608
  267.0 8.5 %copy-start.17 = (s32[128,8]{0,1:T(8,128)S(1)}, s32[128,8]{0,1:T(8,128)}, u32[]{:S(2)}) copy-start(s32[128,8]{0,1:T(8,128)} %param.9) | copy-start | bytes 12292
  267.0 8.6 %slice-start.2 = ((s8[9175040]{0:T(1024)(128)(4,1)}), s8[786432]{0:T(1024)(128)(4,1)S(1)}, s32[]{:S(2)}) async-start(s8[9175040]{0:T(1024)(128)(4,1)} %bitcast.101), calls=%async_computation.4 | async-start | bytes 1572864
  275.0 18.6 %collective-permute-start.8 = (bf16[8,80,3584]{2,1,0:T(8,128)(2,1)}, bf16[8,80,3584]{2,1,0:T(8,128)(2,1)}, u32[]{:S(2)}, u32[]{:S(2)}) collective-permute-start(bf16[8,80,3584]{2,1,0:T(8,128)(2,1)} %bitcast.113), channel_id=1, source_target_pairs={{0,1},{1,0},{2,3},{3,2},{4,5},{5,4},{6,7},{7,6},{8,9},{9,8},{10,11... | collective-permute-start | bytes 13762568 | tf_op jit(solution)/shard_map/ppermute | solution.py:12
  275.6 18.0 %copy-start.10 = (bf16[640,3584]{1,0:T(8,128)(2,1)S(1)}, bf16[640,3584]{1,0:T(8,128)(2,1)}, u32[]{:S(2)}) copy-start(bf16[640,3584]{1,0:T(8,128)(2,1)} %get-tuple-element.15) | copy-start | bytes 13762564
  293.6 14.5 %slice-start.6 = ((s8[9175040]{0:T(1024)(128)(4,1)}), s8[4194304]{0:T(1024)(128)(4,1)S(1)}, s32[]{:S(2)}) async-start(s8[9175040]{0:T(1024)(128)(4,1)} %bitcast.108), calls=%async_computation.8 | async-start | bytes 8388608
  293.6 14.5 %slice-start.7 = ((s8[9175040]{0:T(1024)(128)(4,1)}), s8[4194304]{0:T(1024)(128)(4,1)S(1)}, s32[]{:S(2)}) async-start(s8[9175040]{0:T(1024)(128)(4,1)} %bitcast.108), calls=%async_computation.9 | async-start | bytes 8388608
  300.3 7.8 %slice-start.8 = ((s8[9175040]{0:T(1024)(128)(4,1)}), s8[786432]{0:T(1024)(128)(4,1)S(1)}, s32[]{:S(2)}) async-start(s8[9175040]{0:T(1024)(128)(4,1)} %bitcast.108), calls=%async_computation.10 | async-start | bytes 1572864
  304.3 19.3 %copy-start.3 = (bf16[4,2,2,32,3584]{4,3,2,1,0:T(8,128)(2,1)}, bf16[4,2,2,32,3584]{4,3,2,1,0:T(8,128)(2,1)S(1)}, u32[]{:S(2)}) copy-start(bf16[4,2,2,32,3584]{4,3,2,1,0:T(8,128)(2,1)S(1)} %get-tuple-element.17) | copy-start | bytes 11010052
  304.3 19.3 %copy-start.5 = (bf16[4,2,2,32,3584]{4,3,2,1,0:T(8,128)(2,1)}, bf16[4,2,2,32,3584]{4,3,2,1,0:T(8,128)(2,1)S(1)}, u32[]{:S(2)}) copy-start(bf16[4,2,2,32,3584]{4,3,2,1,0:T(8,128)(2,1)S(1)} %get-tuple-element.18) | copy-start | bytes 11010052
  306.0 17.8 %copy-start.16 = (pred[32,32]{1,0:T(8,128)(4,1)S(1)}, pred[32,32]{1,0:T(8,128)(4,1)}, u32[]{:S(2)}) copy-start(pred[32,32]{1,0:T(8,128)(4,1)} %copy-done.15) | copy-start | bytes 3076
  306.0 42.4 %collective-permute-start.11 = (bf16[4,2,1,32,3584]{4,3,2,1,0:T(8,128)(2,1)}, bf16[4,2,1,32,3584]{4,3,2,1,0:T(8,128)(2,1)}, u32[]{:S(2)}, u32[]{:S(2)}) collective-permute-start(bf16[4,2,1,32,3584]{4,3,2,1,0:T(8,128)(2,1)} %slice.124), channel_id=1, source_target_pairs={{0,16},{16,0},{1,17},{17,1},{2,18},{18,2},{3,19},{19,3},{4,20},{20... | collective-permute-start | bytes 5505032 | tf_op jit(solution)/shard_map/ppermute | solution.py:12
  307.5 44.3 %collective-permute-start.9 = (bf16[4,1,2,32,3584]{4,3,2,1,0:T(8,128)(2,1)S(1)}, bf16[4,1,2,32,3584]{4,3,2,1,0:T(8,128)(2,1)}, u32[]{:S(2)}, u32[]{:S(2)}) collective-permute-start(bf16[4,1,2,32,3584]{4,3,2,1,0:T(8,128)(2,1)S(1)} %slice.119), channel_id=1, source_target_pairs={{0,2},{1,3},{2,0},{3,1},{4,6},{5,7},{6,4},{7,5},{8,10},{9,11},{10,... | collective-permute-start | bytes 5505032 | tf_op jit(solution)/shard_map/ppermute | solution.py:12
  324.6 70.9 %all-to-all-start.1 = ((f32[32,1,64]{2,1,0:T(1,128)}), f32[32,1,64]{2,1,0:T(1,128)S(1)}, u32[]{:S(2)}, u32[]{:S(2)}) async-start(f32[32,1,64]{2,1,0:T(1,128)} %bitcast.38), calls=%async_computation.1 | async-start | bytes 32768 | tf_op jit(solution)/shard_map/all_to_all | solution.py:134
  327.3 24.5 %copy-start.4 = (bf16[4,2,2,32,3584]{4,3,2,1,0:T(8,128)(2,1)S(1)}, bf16[4,2,2,32,3584]{4,3,2,1,0:T(8,128)(2,1)}, u32[]{:S(2)}) copy-start(bf16[4,2,2,32,3584]{4,3,2,1,0:T(8,128)(2,1)} %copy-done.3) | copy-start | bytes 11010052
  348.4 31.6 %slice-start.3 = ((s8[9175040]{0:T(1024)(128)(4,1)}), s8[4194304]{0:T(1024)(128)(4,1)S(1)}, s32[]{:S(2)}) async-start(s8[9175040]{0:T(1024)(128)(4,1)} %bitcast.104), calls=%async_computation.5 | async-start | bytes 8388608
  351.2 28.9 %slice-start.4 = ((s8[9175040]{0:T(1024)(128)(4,1)}), s8[4194304]{0:T(1024)(128)(4,1)S(1)}, s32[]{:S(2)}) async-start(s8[9175040]{0:T(1024)(128)(4,1)} %bitcast.104), calls=%async_computation.6 | async-start | bytes 8388608
  351.2 21.5 %collective-permute-start.12 = (bf16[4,1,1,32,3584]{4,3,2,1,0:T(8,128)(2,1)S(1)}, bf16[4,1,1,32,3584]{4,3,2,1,0:T(8,128)(2,1)S(1)}, u32[]{:S(2)}, u32[]{:S(2)}) collective-permute-start(bf16[4,1,1,32,3584]{4,3,2,1,0:T(8,128)(2,1)S(1)} %slice.126), channel_id=1, source_target_pairs={{0,2},{1,3},{2,0},{3,1},{4,6},{5,7},{6,4},{7,5},{8,10},{9,11},{10,... | collective-permute-start | bytes 2752520 | tf_op jit(solution)/shard_map/ppermute | solution.py:12
  354.1 25.9 %slice-start.5 = ((s8[9175040]{0:T(1024)(128)(4,1)}), s8[786432]{0:T(1024)(128)(4,1)S(1)}, s32[]{:S(2)}) async-start(s8[9175040]{0:T(1024)(128)(4,1)} %bitcast.104), calls=%async_computation.7 | async-start | bytes 1572864
  354.2 21.1 %collective-permute-start.10 = (bf16[4,1,1,32,3584]{4,3,2,1,0:T(8,128)(2,1)S(1)}, bf16[4,1,1,32,3584]{4,3,2,1,0:T(8,128)(2,1)S(1)}, u32[]{:S(2)}, u32[]{:S(2)}) collective-permute-start(bf16[4,1,1,32,3584]{4,3,2,1,0:T(8,128)(2,1)S(1)} %slice.121), channel_id=1, source_target_pairs={{0,16},{16,0},{1,17},{17,1},{2,18},{18,2},{3,19},{19,3},{4,20},{20... | collective-permute-start | bytes 2752520 | tf_op jit(solution)/shard_map/ppermute | solution.py:12
  376.5 19.7 %collective-permute-start.13 = (bf16[64,3584]{1,0:T(8,128)(2,1)}, bf16[64,3584]{1,0:T(8,128)(2,1)S(1)}, u32[]{:S(2)}, u32[]{:S(2)}) collective-permute-start(bf16[64,3584]{1,0:T(8,128)(2,1)} %get-tuple-element.19), channel_id=1, source_target_pairs={{0,4},{1,5},{2,6},{3,7},{4,0},{5,1},{6,2},{7,3},{8,12},{9,13},{10,... | collective-permute-start | bytes 1376264 | tf_op jit(solution)/shard_map/ppermute | solution.py:12
  376.6 23.2 %collective-permute-start.15 = (bf16[64,3584]{1,0:T(8,128)(2,1)}, bf16[64,3584]{1,0:T(8,128)(2,1)}, u32[]{:S(2)}, u32[]{:S(2)}) collective-permute-start(bf16[64,3584]{1,0:T(8,128)(2,1)} %get-tuple-element.20), channel_id=1, source_target_pairs={{0,12},{1,13},{2,14},{3,15},{4,8},{5,9},{6,10},{7,11},{8,4},{9,5},... | collective-permute-start | bytes 1376264 | tf_op jit(solution)/shard_map/ppermute | solution.py:12
  378.1 39.7 %collective-permute-start.14 = (bf16[64,3584]{1,0:T(8,128)(2,1)}, bf16[64,3584]{1,0:T(8,128)(2,1)}, u32[]{:S(2)}, u32[]{:S(2)}) collective-permute-start(bf16[64,3584]{1,0:T(8,128)(2,1)} %get-tuple-element.21), channel_id=1, source_target_pairs={{0,8},{1,9},{2,10},{3,11},{4,12},{5,13},{6,14},{7,15},{8,0},{9,1},... | collective-permute-start | bytes 1376264 | tf_op jit(solution)/shard_map/ppermute | solution.py:12
  380.0 39.9 %copy-start.1 = (bf16[128,3584]{1,0:T(8,128)(2,1)S(1)}, bf16[128,3584]{1,0:T(8,128)(2,1)}, u32[]{:S(2)}) copy-start(bf16[128,3584]{1,0:T(8,128)(2,1)} %param.7) | copy-start | bytes 2752516
